TPU v7x, 32 devices: a whole 2x2x4 slice. The times are simulated.
32 devices in a mesh: rve: 2 (over x), gx: 16 (over z, y, core).
Axes of the slice: x: 2, y: 2, z: 4, core: 2. Of those that a mesh axis runs over, the one named last changes fastest.
Arguments:
- tokens: bfloat16 [32, 16, 128, 128], P(('rve', 'gx')), parts along dimension 0, may hold values from -16 to 16
- cotangent: bfloat16 [32, 16, 128, 128], P(('rve', 'gx')), parts along dimension 0, may hold values from -6 to 6
- offsets: int32 [3], replicated, may hold values from 1 to 7
- norm_gain: float32 [128], replicated, may hold values from 0.5 to 1.5
- qkv_weight: bfloat16 [128, 384], replicated, may hold values from -2.5 to 2.5
- proj_weight: bfloat16 [128, 128], replicated, may hold values from -0.5 to 0.5
Outputs:
- grad_tokens: bfloat16 [32, 16, 128, 128], P(('rve', 'gx')), parts along dimension 0
- grad_qkv: float32 [256, 384], P('rve'), parts along dimension 0
- grad_proj: float32 [256, 128], P('rve'), parts along dimension 0
- grad_gain: float32 [256], P('rve'), parts along dimension 0
There are 2 independent parts, one for each index of `rve`. A program takes and returns all parts, laid end to end along the dimension named above; an argument that names none is the same for every part. Nothing has to cross between parts.
All inputs are finite; a program needn't handle non-finite values.
Results may differ from a plain program's by a relative error of at most 0.012.
The roundings to bfloat16 on the way count: a program that leaves them out, or rounds other values in their place, can miss the bound.
Values may be sent and summed in bfloat16 or wider, within the bound.
A program may use at most 64 MiB of HBM per device.

v0:
```python
import jax
import jax.numpy as jnp
from jax import lax
from jax.sharding import PartitionSpec as P

H = 4


epsilon = 1e-05


def swapped(value, axis, bit):
    return lax.ppermute(value, axis, [(i, i ^ 1 << bit) for i in range(lax.axis_size(axis))])


def from_behind(value, axis, by):
    count = lax.axis_size(axis)
    return lax.ppermute(value, axis, [(i, (i + by) % count) for i in range(count)])


def layer_norm(inputs, norm_gain):
    values = inputs.astype(jnp.float32)
    centre = values - jnp.mean(values, -1, keepdims=True)
    inv_std = lax.rsqrt(jnp.mean(centre * centre, -1, keepdims=True) + epsilon)
    scaled = centre * inv_std
    return ((scaled * norm_gain).astype(jnp.bfloat16), scaled, inv_std)


def layer_norm_back(grad_norm, scaled, inv_std, norm_gain):
    grad_hat = grad_norm * norm_gain
    return inv_std * (
        grad_hat
        - jnp.mean(grad_hat, -1, keepdims=True)
        - scaled * jnp.mean(grad_hat * scaled, -1, keepdims=True)
    )


def band_gather(own_rows):
    device_pos = lax.axis_index("gx")
    gathered = own_rows
    for bit_pos in range(3):
        partner = swapped(gathered, "gx", bit_pos)
        high_bit = device_pos >> bit_pos & 1 == 1
        gathered = jnp.where(
            high_bit,
            jnp.concatenate([partner, gathered], 1),
            jnp.concatenate([gathered, partner], 1),
        )
    return gathered


def band_reduce(band_terms):
    device_pos = lax.axis_index("gx")
    collected = band_terms
    for bit_pos in (2, 1, 0):
        half_len = collected.shape[1] // 2
        lower_half = collected[:, :half_len]
        upper_half = collected[:, half_len:]
        high_bit = device_pos >> bit_pos & 1 == 1
        kept_part = jnp.where(high_bit, upper_half, lower_half)
        sent_part = jnp.where(high_bit, lower_half, upper_half)
        collected = kept_part + swapped(sent_part.astype(jnp.bfloat16), "gx", bit_pos).astype(
            sent_part.dtype
        )
    return collected


def attend_back(queries, keyval, grad_out, head_count):
    win_count, query_rows, features = queries.shape
    key_rows = keyval.shape[1]
    head_dim = features // head_count
    factor = head_dim ** (-0.5)
    query_heads = queries.reshape(win_count, query_rows, head_count, head_dim)
    key_heads = keyval[..., :features].reshape(win_count, key_rows, head_count, head_dim)
    value_heads = keyval[..., features:].reshape(win_count, key_rows, head_count, head_dim)
    grad_heads = grad_out.reshape(win_count, query_rows, head_count, head_dim)
    scores = (
        jnp.einsum("wqhd,wkhd->whqk", query_heads, key_heads, preferred_element_type=jnp.float32)
        * factor
    )
    exponent = jnp.exp(scores - jnp.max(scores, -1, keepdims=True))
    prob_weights = exponent / jnp.sum(exponent, -1, keepdims=True)
    prob_bf = prob_weights.astype(jnp.bfloat16)
    attended = (
        jnp.einsum("whqk,wkhd->wqhd", prob_bf, value_heads, preferred_element_type=jnp.float32)
        .astype(jnp.bfloat16)
        .reshape(win_count, query_rows, features)
    )
    grad_value = jnp.einsum(
        "whqk,wqhd->wkhd", prob_bf, grad_heads, preferred_element_type=jnp.float32
    )
    grad_prob = jnp.einsum(
        "wqhd,wkhd->whqk", grad_heads, value_heads, preferred_element_type=jnp.float32
    )
    grad_score = (
        prob_weights * (grad_prob - jnp.sum(prob_weights * grad_prob, -1, keepdims=True)) * factor
    ).astype(jnp.bfloat16)
    grad_query = (
        jnp.einsum("whqk,wkhd->wqhd", grad_score, key_heads, preferred_element_type=jnp.float32)
        .astype(jnp.bfloat16)
        .reshape(win_count, query_rows, features)
    )
    grad_key = jnp.einsum(
        "whqk,wqhd->wkhd", grad_score, query_heads, preferred_element_type=jnp.float32
    )
    grad_kv = jnp.concatenate(
        [
            grad_key.reshape(win_count, key_rows, features),
            grad_value.reshape(win_count, key_rows, features),
        ],
        -1,
    )
    return (attended, grad_query, grad_kv)


def per_device(tokens, cotangent, offsets, norm_gain, qkv_weight, proj_weight):
    features = tokens.shape[-1]
    extent_two = tokens.shape[1]
    extent_three = tokens.shape[2]
    stacked = jnp.stack([tokens, cotangent])
    stacked = jnp.roll(stacked, -offsets[1], axis=2)
    stacked = jnp.roll(stacked, -offsets[2], axis=3)
    for bit_pos in range(3):
        shifted = from_behind(stacked, "gx", -(1 << bit_pos))
        chosen = offsets[0] >> bit_pos & 1 == 1
        stacked = jnp.where(chosen, shifted, stacked)
    kv_weight = qkv_weight[:, features:]
    kv_trans = kv_weight.astype(jnp.float32).T
    query_trans = qkv_weight[:, :features].T
    proj_trans = proj_weight.T
    initial = (
        jnp.zeros((features, 3 * features), jnp.float32),
        jnp.zeros((features, features), jnp.float32),
        jnp.zeros((features,), jnp.float32),
    )

    def to_windows(grid_field):
        blocked = grid_field.reshape(extent_two // 8, 8, extent_three // 8, 8, features)
        return blocked.transpose(0, 2, 1, 3, 4).reshape(-1, 8, 64, features)

    def group_step(totals, blocks):
        acc_qkv, acc_proj, acc_gain = totals
        own_tokens, own_cot = blocks
        win_count, query_rows = (own_tokens.shape[0], own_tokens.shape[1])
        normed, scaled, inv_std = layer_norm(own_tokens, norm_gain)
        flat_normed = normed.reshape(-1, features)
        projected = (
            jnp.dot(flat_normed, qkv_weight, preferred_element_type=jnp.float32)
            .astype(jnp.bfloat16)
            .reshape(win_count, query_rows, 3 * features)
        )
        queries = projected[..., :features]
        band_tokens = band_gather(own_tokens)
        band_normed = layer_norm(band_tokens, norm_gain)[0].reshape(-1, features)
        keyval = (
            jnp.dot(band_normed, kv_weight, preferred_element_type=jnp.float32)
            .astype(jnp.bfloat16)
            .reshape(win_count, 8 * query_rows, 2 * features)
        )
        flat_cot = own_cot.reshape(-1, features)
        grad_out = (
            jnp.dot(flat_cot, proj_trans, preferred_element_type=jnp.float32)
            .astype(jnp.bfloat16)
            .reshape(win_count, query_rows, features)
        )
        attended, grad_query, grad_kv = attend_back(queries, keyval, grad_out, H)
        acc_proj = acc_proj + jnp.dot(
            attended.reshape(-1, features).T, flat_cot, preferred_element_type=jnp.float32
        )
        flat_grad_query = grad_query.reshape(-1, features)
        grad_q_w = jnp.dot(flat_normed.T, flat_grad_query, preferred_element_type=jnp.float32)
        grad_norm = jnp.dot(flat_grad_query, query_trans, preferred_element_type=jnp.float32)
        flat_kv = grad_kv.reshape(-1, 2 * features)
        grad_kv_w = jnp.dot(
            band_normed.astype(jnp.float32).T, flat_kv, precision=lax.Precision.HIGHEST
        )
        band_terms = jnp.dot(flat_kv, kv_trans, precision=lax.Precision.HIGHEST).reshape(
            win_count, 8 * query_rows, features
        )
        grad_norm = grad_norm + band_reduce(band_terms).reshape(-1, features)
        flat_scaled = scaled.reshape(-1, features)
        acc_qkv = acc_qkv + jnp.concatenate([grad_q_w, grad_kv_w], 1)
        acc_gain = acc_gain + jnp.sum(grad_norm * flat_scaled, 0)
        grad_rows = layer_norm_back(grad_norm, flat_scaled, inv_std.reshape(-1, 1), norm_gain)
        grad_group = (
            (flat_cot.astype(jnp.float32) + grad_rows)
            .astype(jnp.bfloat16)
            .reshape(win_count, query_rows, features)
        )
        return ((acc_qkv, acc_proj, acc_gain), grad_group)

    totals, grad_groups = lax.scan(
        group_step, initial, (to_windows(stacked[0]), to_windows(stacked[1]))
    )
    blocked = grad_groups.reshape(extent_two // 8, extent_three // 8, 8, 8, features)
    grad_field = blocked.transpose(0, 2, 1, 3, 4).reshape(1, extent_two, extent_three, features)
    for bit_pos in range(3):
        shifted = from_behind(grad_field, "gx", 1 << bit_pos)
        chosen = offsets[0] >> bit_pos & 1 == 1
        grad_field = jnp.where(chosen, shifted, grad_field)
    grad_field = jnp.roll(grad_field, offsets[1], axis=1)
    grad_field = jnp.roll(grad_field, offsets[2], axis=2)
    summed = lax.psum((totals[0], totals[1], totals[2]), "gx")
    norm_scale = (lax.axis_size("gx") * extent_two * extent_three) ** (-0.5)
    return (grad_field, summed[0] * norm_scale, summed[1] * norm_scale, summed[2] * norm_scale)


def solution(mesh):
    in_specs = (
        P(("rve", "gx"), None, None, None),
        P(("rve", "gx"), None, None, None),
        P(),
        P(),
        P(),
        P(),
    )
    out_specs = (P(("rve", "gx"), None, None, None), P("rve", None), P("rve", None), P("rve"))
    return jax.shard_map(
        per_device, mesh=mesh, in_specs=in_specs, out_specs=out_specs, check_vma=False
    )
```

profile of v0, /device:TPU:1, one launch (start us, length us, event | category | flops | bytes accessed | tf_op | source)
XLA Modules:
  0.0 668.5 jit_solution(6381331876810162120)
XLA Ops:
  14.3 14.4 %collective-permute-done.6 = bf16[2,1,16,128,128]{4,3,2,1,0:T(8,128)(2,1)S(1)} collective-permute-done((bf16[2,1,16,128,128]{4,3,2,1,0:T(8,128)(2,1)S(1)}, bf16[2,1,16,128,128]{4,3,2,1,0:T(8,128)(2,1)S(1)}, u32[]{:S(2)}, u32[]{:S(2)}) %collective-permute-start.6) | collective-permute-done | bytes 1048608 | tf_op jit(solution)/shard_map/ppermute | solution.py:18
  29.7 7.0 %collective-permute-start.7 = (bf16[2,1,16,128,128]{4,3,2,1,0:T(8,128)(2,1)S(1)}, bf16[2,1,16,128,128]{4,3,2,1,0:T(8,128)(2,1)S(1)}, u32[]{:S(2)}, u32[]{:S(2)}) collective-permute-start(bf16[2,1,16,128,128]{4,3,2,1,0:T(8,128)(2,1)S(1)} %broadcast_select_fusion.1), channel_id=1, source_target_pairs={{0,14},{1,15},{2,0},{3,1},{4,2},{5,3},{6,4},{7,5},{8,6},{9,7},{10,... | collective-permute-start | bytes 3145736 | tf_op jit(solution)/shard_map/ppermute | solution.py:18
  37.3 18.9 %collective-permute-done.7 = bf16[2,1,16,128,128]{4,3,2,1,0:T(8,128)(2,1)S(1)} collective-permute-done((bf16[2,1,16,128,128]{4,3,2,1,0:T(8,128)(2,1)S(1)}, bf16[2,1,16,128,128]{4,3,2,1,0:T(8,128)(2,1)S(1)}, u32[]{:S(2)}, u32[]{:S(2)}) %collective-permute-start.7) | collective-permute-done | bytes 1048608 | tf_op jit(solution)/shard_map/ppermute | solution.py:18
  64.1 17.2 %collective-permute-done.8 = bf16[2,1,16,128,128]{4,3,2,1,0:T(8,128)(2,1)S(1)} collective-permute-done((bf16[2,1,16,128,128]{4,3,2,1,0:T(8,128)(2,1)S(1)}, bf16[2,1,16,128,128]{4,3,2,1,0:T(8,128)(2,1)S(1)}, u32[]{:S(2)}, u32[]{:S(2)}) %collective-permute-start.8) | collective-permute-done | bytes 1048608 | tf_op jit(solution)/shard_map/ppermute | solution.py:18
  82.6 466.0 %while.17 = (s32[]{:T(128)}, f32[128,384]{1,0:T(8,128)}, f32[128,128]{1,0:T(8,128)}, f32[128]{0:T(128)}, bf16[4,8,64,128]{3,2,1,0:T(8,128)(2,1)}, /*index=5*/bf1...) while((s32[]{:T(128)}, f32[128,384]{1,0:T(8,128)}, ...), condition=%wide.region_11.12_spmd.clone, body=%wide.region_0.11_spmd.clone.sunk | while | flops 4070566144 | bytes 146137328 | solution.py:192
  97.3 7.4 %collective-permute-done.2 = bf16[8,256,128]{2,1,0:T(8,128)(2,1)S(1)} collective-permute-done((bf16[8,256,128]{2,1,0:T(8,128)(2,1)S(1)}, bf16[8,256,128]{2,1,0:T(8,128)(2,1)S(1)}, u32[]{:S(2)}, u32[]{:S(2)}) %collective-permute-start.2) | collective-permute-done | bytes 524320 | tf_op jit(solution)/shard_map/while/body/eval_jaxpr/ppermute | solution.py:13
  121.2 18.0 %fusion.159 = bf16[8,64,4,32]{1,3,2,0:T(8,128)(2,1)} fusion(bf16[8,512,4,32]{1,3,2,0:T(8,128)(2,1)S(1)} %bitcast.193, f32[8,4,64,512]{3,2,1,0:T(8,128)} %fusion.156, f32[8,4,64,512]{3,2,1,0:T(8,128)} %get-tuple-element.270, f32[8,4,64]{2,1,0:T(4,128)S(1)} %get-tuple-element.271), kind=kOutput, calls=%fused_computation.29.clone.1 | convolution fusion | flops 74516992 | bytes 9576448 | tf_op jit(solution)/shard_map/while/body/eval_jaxpr/whqk,wkhd->wqhd/dot_general | solution.py:99
  139.2 18.7 %fusion.157 = f32[8,4,32,512]{3,2,1,0:T(8,128)} fusion(bf16[8,64,4,32]{1,3,2,0:T(8,128)(2,1)S(1)} %bitcast.200, f32[8,4,64,512]{3,2,1,0:T(8,128)} %fusion.156, f32[8,4,64,512]{3,2,1,0:T(8,128)} %get-tuple-element.270, f32[8,4,64]{2,1,0:T(4,128)S(1)} %get-tuple-element.271), kind=kOutput, calls=%fused_computation.12.clone.1 | convolution fusion | flops 74451456 | bytes 10625024 | tf_op jit(solution)/shard_map/while/body/eval_jaxpr/whqk,wqhd->wkhd/dot_general | solution.py:103
  179.4 6.3 collective-permute-done.3
  214.0 7.2 %collective-permute-done.2 = bf16[8,256,128]{2,1,0:T(8,128)(2,1)S(1)} collective-permute-done((bf16[8,256,128]{2,1,0:T(8,128)(2,1)S(1)}, bf16[8,256,128]{2,1,0:T(8,128)(2,1)S(1)}, u32[]{:S(2)}, u32[]{:S(2)}) %collective-permute-start.2) | collective-permute-done | bytes 524320 | tf_op jit(solution)/shard_map/while/body/eval_jaxpr/ppermute | solution.py:13
  237.6 18.0 %fusion.159 = bf16[8,64,4,32]{1,3,2,0:T(8,128)(2,1)} fusion(bf16[8,512,4,32]{1,3,2,0:T(8,128)(2,1)S(1)} %bitcast.193, f32[8,4,64,512]{3,2,1,0:T(8,128)} %fusion.156, f32[8,4,64,512]{3,2,1,0:T(8,128)} %get-tuple-element.270, f32[8,4,64]{2,1,0:T(4,128)S(1)} %get-tuple-element.271), kind=kOutput, calls=%fused_computation.29.clone.1 | convolution fusion | flops 74516992 | bytes 9576448 | tf_op jit(solution)/shard_map/while/body/eval_jaxpr/whqk,wkhd->wqhd/dot_general | solution.py:99
  255.6 18.7 %fusion.157 = f32[8,4,32,512]{3,2,1,0:T(8,128)} fusion(bf16[8,64,4,32]{1,3,2,0:T(8,128)(2,1)S(1)} %bitcast.200, f32[8,4,64,512]{3,2,1,0:T(8,128)} %fusion.156, f32[8,4,64,512]{3,2,1,0:T(8,128)} %get-tuple-element.270, f32[8,4,64]{2,1,0:T(4,128)S(1)} %get-tuple-element.271), kind=kOutput, calls=%fused_computation.12.clone.1 | convolution fusion | flops 74451456 | bytes 10625024 | tf_op jit(solution)/shard_map/while/body/eval_jaxpr/whqk,wqhd->wkhd/dot_general | solution.py:103
  295.8 6.3 collective-permute-done.3
  330.4 7.2 %collective-permute-done.2 = bf16[8,256,128]{2,1,0:T(8,128)(2,1)S(1)} collective-permute-done((bf16[8,256,128]{2,1,0:T(8,128)(2,1)S(1)}, bf16[8,256,128]{2,1,0:T(8,128)(2,1)S(1)}, u32[]{:S(2)}, u32[]{:S(2)}) %collective-permute-start.2) | collective-permute-done | bytes 524320 | tf_op jit(solution)/shard_map/while/body/eval_jaxpr/ppermute | solution.py:13
  354.0 18.0 %fusion.159 = bf16[8,64,4,32]{1,3,2,0:T(8,128)(2,1)} fusion(bf16[8,512,4,32]{1,3,2,0:T(8,128)(2,1)S(1)} %bitcast.193, f32[8,4,64,512]{3,2,1,0:T(8,128)} %fusion.156, f32[8,4,64,512]{3,2,1,0:T(8,128)} %get-tuple-element.270, f32[8,4,64]{2,1,0:T(4,128)S(1)} %get-tuple-element.271), kind=kOutput, calls=%fused_computation.29.clone.1 | convolution fusion | flops 74516992 | bytes 9576448 | tf_op jit(solution)/shard_map/while/body/eval_jaxpr/whqk,wkhd->wqhd/dot_general | solution.py:99
  372.0 18.7 %fusion.157 = f32[8,4,32,512]{3,2,1,0:T(8,128)} fusion(bf16[8,64,4,32]{1,3,2,0:T(8,128)(2,1)S(1)} %bitcast.200, f32[8,4,64,512]{3,2,1,0:T(8,128)} %fusion.156, f32[8,4,64,512]{3,2,1,0:T(8,128)} %get-tuple-element.270, f32[8,4,64]{2,1,0:T(4,128)S(1)} %get-tuple-element.271), kind=kOutput, calls=%fused_computation.12.clone.1 | convolution fusion | flops 74451456 | bytes 10625024 | tf_op jit(solution)/shard_map/while/body/eval_jaxpr/whqk,wqhd->wkhd/dot_general | solution.py:103
  412.2 6.3 collective-permute-done.3
  446.7 7.2 %collective-permute-done.2 = bf16[8,256,128]{2,1,0:T(8,128)(2,1)S(1)} collective-permute-done((bf16[8,256,128]{2,1,0:T(8,128)(2,1)S(1)}, bf16[8,256,128]{2,1,0:T(8,128)(2,1)S(1)}, u32[]{:S(2)}, u32[]{:S(2)}) %collective-permute-start.2) | collective-permute-done | bytes 524320 | tf_op jit(solution)/shard_map/while/body/eval_jaxpr/ppermute | solution.py:13
  470.4 18.0 %fusion.159 = bf16[8,64,4,32]{1,3,2,0:T(8,128)(2,1)} fusion(bf16[8,512,4,32]{1,3,2,0:T(8,128)(2,1)S(1)} %bitcast.193, f32[8,4,64,512]{3,2,1,0:T(8,128)} %fusion.156, f32[8,4,64,512]{3,2,1,0:T(8,128)} %get-tuple-element.270, f32[8,4,64]{2,1,0:T(4,128)S(1)} %get-tuple-element.271), kind=kOutput, calls=%fused_computation.29.clone.1 | convolution fusion | flops 74516992 | bytes 9576448 | tf_op jit(solution)/shard_map/while/body/eval_jaxpr/whqk,wkhd->wqhd/dot_general | solution.py:99
  488.4 18.7 %fusion.157 = f32[8,4,32,512]{3,2,1,0:T(8,128)} fusion(bf16[8,64,4,32]{1,3,2,0:T(8,128)(2,1)S(1)} %bitcast.200, f32[8,4,64,512]{3,2,1,0:T(8,128)} %fusion.156, f32[8,4,64,512]{3,2,1,0:T(8,128)} %get-tuple-element.270, f32[8,4,64]{2,1,0:T(4,128)S(1)} %get-tuple-element.271), kind=kOutput, calls=%fused_computation.12.clone.1 | convolution fusion | flops 74451456 | bytes 10625024 | tf_op jit(solution)/shard_map/while/body/eval_jaxpr/whqk,wqhd->wkhd/dot_general | solution.py:103
  528.6 6.3 collective-permute-done.3
  550.9 6.1 collective-permute-done.9
  560.3 33.4 %psum.23 = f32[128]{0:T(128)S(1)} all-reduce(f32[128]{0:T(128)S(1)} %copy-done.24), channel_id=1, replica_groups=mesh['rve'=2,'gx'=16] {'gx'}, use_global_device_ids=true, to_apply=%region_14.15 | all-reduce | flops 128 | bytes 1024 | tf_op jit(solution)/shard_map/psum | solution.py:203
  594.3 62.8 %all-reduce.3.cloned.1.call-done = (f32[128,384]{1,0:T(8,128)}, f32[128,128]{1,0:T(8,128)}) async-done(((f32[128,384]{1,0:T(8,128)}, f32[128,128]{1,0:T(8,128)}), (f32[128,384]{1,0:T(8,128)}, f32[128,128]{1,0:T(8,128)})) %all-reduce.3.cloned.1.call-update) | async-done | bytes 262160 | tf_op jit(solution)/shard_map/psum | solution.py:203
  (481 shorter events, 284.3 us)
Async XLA Ops:
  7.2 649.9 %all-reduce.3.cloned.1.call-start = ((), (), s32[]{:S(2)}) async-start(), calls=%async_computation | async-start | bytes 524288 | tf_op jit(solution)/shard_map/psum | solution.py:203
  13.6 15.2 %collective-permute-start.6 = (bf16[2,1,16,128,128]{4,3,2,1,0:T(8,128)(2,1)S(1)}, bf16[2,1,16,128,128]{4,3,2,1,0:T(8,128)(2,1)S(1)}, u32[]{:S(2)}, u32[]{:S(2)}) collective-permute-start(bf16[2,1,16,128,128]{4,3,2,1,0:T(8,128)(2,1)S(1)} %fusion.55), channel_id=1, source_target_pairs={{0,15},{1,0},{2,1},{3,2},{4,3},{5,4},{6,5},{7,6},{8,7},{9,8},{10,9... | collective-permute-start | bytes 3145736 | tf_op jit(solution)/shard_map/ppermute | solution.py:18
  29.7 26.5 %collective-permute-start.7 = (bf16[2,1,16,128,128]{4,3,2,1,0:T(8,128)(2,1)S(1)}, bf16[2,1,16,128,128]{4,3,2,1,0:T(8,128)(2,1)S(1)}, u32[]{:S(2)}, u32[]{:S(2)}) collective-permute-start(bf16[2,1,16,128,128]{4,3,2,1,0:T(8,128)(2,1)S(1)} %broadcast_select_fusion.1), channel_id=1, source_target_pairs={{0,14},{1,15},{2,0},{3,1},{4,2},{5,3},{6,4},{7,5},{8,6},{9,7},{10,... | collective-permute-start | bytes 3145736 | tf_op jit(solution)/shard_map/ppermute | solution.py:18
  56.3 25.0 %collective-permute-start.8 = (bf16[2,1,16,128,128]{4,3,2,1,0:T(8,128)(2,1)S(1)}, bf16[2,1,16,128,128]{4,3,2,1,0:T(8,128)(2,1)S(1)}, u32[]{:S(2)}, u32[]{:S(2)}) collective-permute-start(bf16[2,1,16,128,128]{4,3,2,1,0:T(8,128)(2,1)S(1)} %broadcast_select_fusion.2), channel_id=1, source_target_pairs={{0,12},{1,13},{2,14},{3,15},{4,0},{5,1},{6,2},{7,3},{8,4},{9,5},{1... | collective-permute-start | bytes 3145736 | tf_op jit(solution)/shard_map/ppermute | solution.py:18
  84.8 7.6 %collective-permute-start.1 = (bf16[8,128,128]{2,1,0:T(8,128)(2,1)S(1)}, bf16[8,128,128]{2,1,0:T(8,128)(2,1)S(1)}, u32[]{:S(2)}, u32[]{:S(2)}) collective-permute-start(bf16[8,128,128]{2,1,0:T(8,128)(2,1)S(1)} %maximum_select_fusion.6), channel_id=1, source_target_pairs={{0,2},{1,3},{2,0},{3,1},{4,6},{5,7},{6,4},{7,5},{8,10},{9,11},{10,... | collective-permute-start | bytes 786440 | tf_op jit(solution)/shard_map/while/body/eval_jaxpr/ppermute | solution.py:13
  92.5 12.3 %collective-permute-start.2 = (bf16[8,256,128]{2,1,0:T(8,128)(2,1)S(1)}, bf16[8,256,128]{2,1,0:T(8,128)(2,1)S(1)}, u32[]{:S(2)}, u32[]{:S(2)}) collective-permute-start(bf16[8,256,128]{2,1,0:T(8,128)(2,1)S(1)} %maximum_select_fusion.7), channel_id=1, source_target_pairs={{0,4},{1,5},{2,6},{3,7},{4,0},{5,1},{6,2},{7,3},{8,12},{9,13},{10,... | collective-permute-start | bytes 1572872 | tf_op jit(solution)/shard_map/while/body/eval_jaxpr/ppermute | solution.py:13
  174.4 11.4 %collective-permute-start.3 = (bf16[8,256,128]{2,1,0:T(8,128)(2,1)S(1)}, bf16[8,256,128]{2,1,0:T(8,128)(2,1)S(1)}, u32[]{:S(2)}, u32[]{:S(2)}) collective-permute-start(bf16[8,256,128]{2,1,0:T(8,128)(2,1)S(1)} %select_convert_fusion.6), channel_id=1, source_target_pairs={{0,4},{1,5},{2,6},{3,7},{4,0},{5,1},{6,2},{7,3},{8,12},{9,13},{10,... | collective-permute-start | bytes 1572872 | tf_op jit(solution)/shard_map/while/body/eval_jaxpr/ppermute | solution.py:13
  186.0 5.3 collective-permute-start.4
  201.1 7.6 %collective-permute-start.1 = (bf16[8,128,128]{2,1,0:T(8,128)(2,1)S(1)}, bf16[8,128,128]{2,1,0:T(8,128)(2,1)S(1)}, u32[]{:S(2)}, u32[]{:S(2)}) collective-permute-start(bf16[8,128,128]{2,1,0:T(8,128)(2,1)S(1)} %maximum_select_fusion.6), channel_id=1, source_target_pairs={{0,2},{1,3},{2,0},{3,1},{4,6},{5,7},{6,4},{7,5},{8,10},{9,11},{10,... | collective-permute-start | bytes 786440 | tf_op jit(solution)/shard_map/while/body/eval_jaxpr/ppermute | solution.py:13
  208.9 12.3 %collective-permute-start.2 = (bf16[8,256,128]{2,1,0:T(8,128)(2,1)S(1)}, bf16[8,256,128]{2,1,0:T(8,128)(2,1)S(1)}, u32[]{:S(2)}, u32[]{:S(2)}) collective-permute-start(bf16[8,256,128]{2,1,0:T(8,128)(2,1)S(1)} %maximum_select_fusion.7), channel_id=1, source_target_pairs={{0,4},{1,5},{2,6},{3,7},{4,0},{5,1},{6,2},{7,3},{8,12},{9,13},{10,... | collective-permute-start | bytes 1572872 | tf_op jit(solution)/shard_map/while/body/eval_jaxpr/ppermute | solution.py:13
  290.8 11.4 %collective-permute-start.3 = (bf16[8,256,128]{2,1,0:T(8,128)(2,1)S(1)}, bf16[8,256,128]{2,1,0:T(8,128)(2,1)S(1)}, u32[]{:S(2)}, u32[]{:S(2)}) collective-permute-start(bf16[8,256,128]{2,1,0:T(8,128)(2,1)S(1)} %select_convert_fusion.6), channel_id=1, source_target_pairs={{0,4},{1,5},{2,6},{3,7},{4,0},{5,1},{6,2},{7,3},{8,12},{9,13},{10,... | collective-permute-start | bytes 1572872 | tf_op jit(solution)/shard_map/while/body/eval_jaxpr/ppermute | solution.py:13
  302.3 5.3 collective-permute-start.4
  307.7 5.3 collective-permute-start.5
  317.5 7.6 %collective-permute-start.1 = (bf16[8,128,128]{2,1,0:T(8,128)(2,1)S(1)}, bf16[8,128,128]{2,1,0:T(8,128)(2,1)S(1)}, u32[]{:S(2)}, u32[]{:S(2)}) collective-permute-start(bf16[8,128,128]{2,1,0:T(8,128)(2,1)S(1)} %maximum_select_fusion.6), channel_id=1, source_target_pairs={{0,2},{1,3},{2,0},{3,1},{4,6},{5,7},{6,4},{7,5},{8,10},{9,11},{10,... | collective-permute-start | bytes 786440 | tf_op jit(solution)/shard_map/while/body/eval_jaxpr/ppermute | solution.py:13
  325.3 12.3 %collective-permute-start.2 = (bf16[8,256,128]{2,1,0:T(8,128)(2,1)S(1)}, bf16[8,256,128]{2,1,0:T(8,128)(2,1)S(1)}, u32[]{:S(2)}, u32[]{:S(2)}) collective-permute-start(bf16[8,256,128]{2,1,0:T(8,128)(2,1)S(1)} %maximum_select_fusion.7), channel_id=1, source_target_pairs={{0,4},{1,5},{2,6},{3,7},{4,0},{5,1},{6,2},{7,3},{8,12},{9,13},{10,... | collective-permute-start | bytes 1572872 | tf_op jit(solution)/shard_map/while/body/eval_jaxpr/ppermute | solution.py:13
  407.2 11.4 %collective-permute-start.3 = (bf16[8,256,128]{2,1,0:T(8,128)(2,1)S(1)}, bf16[8,256,128]{2,1,0:T(8,128)(2,1)S(1)}, u32[]{:S(2)}, u32[]{:S(2)}) collective-permute-start(bf16[8,256,128]{2,1,0:T(8,128)(2,1)S(1)} %select_convert_fusion.6), channel_id=1, source_target_pairs={{0,4},{1,5},{2,6},{3,7},{4,0},{5,1},{6,2},{7,3},{8,12},{9,13},{10,... | collective-permute-start | bytes 1572872 | tf_op jit(solution)/shard_map/while/body/eval_jaxpr/ppermute | solution.py:13
  418.7 5.3 collective-permute-start.4
  433.9 7.6 %collective-permute-start.1 = (bf16[8,128,128]{2,1,0:T(8,128)(2,1)S(1)}, bf16[8,128,128]{2,1,0:T(8,128)(2,1)S(1)}, u32[]{:S(2)}, u32[]{:S(2)}) collective-permute-start(bf16[8,128,128]{2,1,0:T(8,128)(2,1)S(1)} %maximum_select_fusion.6), channel_id=1, source_target_pairs={{0,2},{1,3},{2,0},{3,1},{4,6},{5,7},{6,4},{7,5},{8,10},{9,11},{10,... | collective-permute-start | bytes 786440 | tf_op jit(solution)/shard_map/while/body/eval_jaxpr/ppermute | solution.py:13
  441.7 12.3 %collective-permute-start.2 = (bf16[8,256,128]{2,1,0:T(8,128)(2,1)S(1)}, bf16[8,256,128]{2,1,0:T(8,128)(2,1)S(1)}, u32[]{:S(2)}, u32[]{:S(2)}) collective-permute-start(bf16[8,256,128]{2,1,0:T(8,128)(2,1)S(1)} %maximum_select_fusion.7), channel_id=1, source_target_pairs={{0,4},{1,5},{2,6},{3,7},{4,0},{5,1},{6,2},{7,3},{8,12},{9,13},{10,... | collective-permute-start | bytes 1572872 | tf_op jit(solution)/shard_map/while/body/eval_jaxpr/ppermute | solution.py:13
  523.5 11.4 %collective-permute-start.3 = (bf16[8,256,128]{2,1,0:T(8,128)(2,1)S(1)}, bf16[8,256,128]{2,1,0:T(8,128)(2,1)S(1)}, u32[]{:S(2)}, u32[]{:S(2)}) collective-permute-start(bf16[8,256,128]{2,1,0:T(8,128)(2,1)S(1)} %select_convert_fusion.6), channel_id=1, source_target_pairs={{0,4},{1,5},{2,6},{3,7},{4,0},{5,1},{6,2},{7,3},{8,12},{9,13},{10,... | collective-permute-start | bytes 1572872 | tf_op jit(solution)/shard_map/while/body/eval_jaxpr/ppermute | solution.py:13
  535.1 5.3 collective-permute-start.4
  549.8 7.2 %collective-permute-start.9 = (bf16[1,16,128,128]{3,2,1,0:T(8,128)(2,1)S(1)}, bf16[1,16,128,128]{3,2,1,0:T(8,128)(2,1)S(1)}, u32[]{:S(2)}, u32[]{:S(2)}) collective-permute-start(bf16[1,16,128,128]{3,2,1,0:T(8,128)(2,1)S(1)} %bitcast.204), channel_id=1, source_target_pairs={{0,1},{1,2},{2,3},{3,4},{4,5},{5,6},{6,7},{7,8},{8,9},{9,10},{10,1... | collective-permute-start | bytes 1572872 | tf_op jit(solution)/shard_map/ppermute | solution.py:18
  557.0 36.6 %collective-permute-start.10 = (bf16[1,16,128,128]{3,2,1,0:T(8,128)(2,1)S(1)}, bf16[1,16,128,128]{3,2,1,0:T(8,128)(2,1)S(1)}, u32[]{:S(2)}, u32[]{:S(2)}) collective-permute-start(bf16[1,16,128,128]{3,2,1,0:T(8,128)(2,1)S(1)} %broadcast_select_fusion.4), channel_id=1, source_target_pairs={{0,2},{1,3},{2,4},{3,5},{4,6},{5,7},{6,8},{7,9},{8,10},{9,11},{10,... | collective-permute-start | bytes 1572872 | tf_op jit(solution)/shard_map/ppermute | solution.py:18
  593.7 66.5 %collective-permute-start.11 = (bf16[1,16,128,128]{3,2,1,0:T(8,128)(2,1)S(1)}, bf16[1,16,128,128]{3,2,1,0:T(8,128)(2,1)S(1)}, u32[]{:S(2)}, u32[]{:S(2)}) collective-permute-start(bf16[1,16,128,128]{3,2,1,0:T(8,128)(2,1)S(1)} %broadcast_select_fusion.5), channel_id=1, source_target_pairs={{0,4},{1,5},{2,6},{3,7},{4,8},{5,9},{6,10},{7,11},{8,12},{9,13},{1... | collective-permute-start | bytes 1572872 | tf_op jit(solution)/shard_map/ppermute | solution.py:18
  (101 other events, 860.4 us)
Sparse Core Ops, SparseCore 0:
  560.4 96.6 all-reduce.2
where the time goes:
time: 671 us; the launch traced here: 668 us
  matrix products  251 us (37%)
  waiting for transfers between devices  214 us (32%)
  local copies, waits for them, and re-layouts  63.7 us (9%)
  other arithmetic  44.7 us (7%)
  starting transfers between devices  38.2 us (6%)
  blocking collectives  33.4 us (5%)
  between operations  21 us (3%)
    ppermute x24, waiting for transfers between devices, swapped(): lax.ppermute(value, axis, [(i, i ^ 1 << bit) for i in range(lax.axis_size...  94.7 us
    dot_general x4, matrix products, attend_back(): jnp.einsum('whqk,wqhd->wkhd', grad_score, query_heads, preferred_element_...  75 us
    dot_general x4, matrix products, attend_back(): jnp.einsum('whqk,wkhd->wqhd', grad_score, key_heads, preferred_element_ty...  72 us
    psum x1, waiting for transfers between devices, per_device(): summed = lax.psum((totals[0], totals[1], totals[2]), 'gx')  62.8 us
    ppermute x6, waiting for transfers between devices, from_behind(): lax.ppermute(value, axis, [(i, (i + by) % count) for i in range(count)])  56.6 us
    psum x1, blocking collectives, per_device(): summed = lax.psum((totals[0], totals[1], totals[2]), 'gx')  33.4 us
    ppermute x24, starting transfers between devices, swapped(): lax.ppermute(value, axis, [(i, i ^ 1 << bit) for i in range(lax.axis_size...  27.4 us
    dot_general x4, matrix products, group_step(): jnp.dot(flat_kv, kv_trans, precision=lax.Precision.HIGHEST)  21.3 us
  transfers between devices with their start and end apart: 31, of which 29 were waited for; matrix products, arithmetic and copies ran while one was open for 9% of the time, Pallas kernels for 0%

commit v1 on v0

v1 whole, which is shorter than its diff:
```python
import jax
import jax.numpy as jnp
from jax import lax
from jax.experimental import pallas as pl
from jax.experimental.pallas import tpu as pltpu
from jax.sharding import PartitionSpec as P

H = 4
W = 8
EPSILON = 1e-05
F32 = jnp.float32
BF16 = jnp.bfloat16


def nn(a, b):
    return lax.dot_general(a, b, (((1,), (0,)), ((), ())), preferred_element_type=F32)


def nt(a, b):
    return lax.dot_general(a, b, (((1,), (1,)), ((), ())), preferred_element_type=F32)


def split_two(value):
    high = value.astype(BF16)
    low = (value - high.astype(F32)).astype(BF16)
    return high, low


def window_kernel(
    offsets_ref, data_ref, gain_ref, qkv_ref, back_ref, proj_t_ref, mask_ref,
    grad_ref, acc_qkv_ref, acc_proj_ref, acc_gain_ref,
    tok_ref, cot_ref, res_ref,
):
    extent_x, _, extent_y = data_ref.shape[:3]
    features = data_ref.shape[-1]
    step = pl.program_id(0)
    per_y = extent_y // W
    first_x = (step // per_y) * W + offsets_ref[0]
    first_y = (step % per_y) * W + offsets_ref[1]

    def place(i, j):
        return lax.rem(first_x + i, extent_x), lax.rem(first_y + j, extent_y)

    for i in range(W):
        for j in range(W):
            at_x, at_y = place(i, j)
            rows = pl.ds((i * W + j) * W, W)
            tok_ref[rows, :] = data_ref[at_x, 0, at_y].astype(F32)
            cot_ref[rows, :] = data_ref[at_x, 1, at_y].astype(F32)

    gain = gain_ref[...]
    values = tok_ref[...]
    centre = values - jnp.mean(values, -1, keepdims=True)
    inv_std = lax.rsqrt(jnp.mean(centre * centre, -1, keepdims=True) + EPSILON)
    scaled = centre * inv_std
    normed = (scaled * gain).astype(BF16)
    cot = cot_ref[...].astype(BF16)
    projected = nn(normed, qkv_ref[...]).astype(BF16)
    queries = projected[:, :features]
    keys = projected[:, features : 2 * features]
    values_bf = projected[:, 2 * features :]
    grad_out = nn(cot, proj_t_ref[...]).astype(BF16)
    keys_t = keys.T
    values_t = values_bf.T

    head_dim = features // H
    factor = head_dim ** (-0.5)
    exp_factor = factor * 1.4426950408889634
    grad_key = jnp.zeros((W * W * W, features), F32)
    grad_value = jnp.zeros((W * W * W, features), F32)
    attended_rows = []
    grad_query_rows = []
    for head in range(H):
        mask = mask_ref[head : head + 1, :]
        head_rows = slice(head * head_dim, (head + 1) * head_dim)
        query_h = queries * mask
        grad_h = grad_out * mask
        scores = nt(keys, query_h)
        exponent = jnp.exp2((scores - jnp.max(scores, 0, keepdims=True)) * exp_factor)
        prob = exponent * (1.0 / jnp.sum(exponent, 0, keepdims=True))
        prob_bf = prob.astype(BF16)
        attended_rows.append(nn(values_t[head_rows], prob_bf).astype(BF16))
        grad_value = grad_value + nn(prob_bf, grad_h)
        grad_prob = nt(values_bf, grad_h)
        row_sum = jnp.sum(prob * grad_prob, 0, keepdims=True)
        grad_score = (prob * (grad_prob - row_sum) * factor).astype(BF16)
        grad_query_rows.append(nn(keys_t[head_rows], grad_score).astype(BF16))
        grad_key = grad_key + nn(grad_score, query_h)

    attended_t = jnp.concatenate(attended_rows, 0)
    grad_query = jnp.concatenate(grad_query_rows, 0).T
    key_high, key_low = split_two(grad_key)
    value_high, value_low = split_two(grad_value)
    terms = jnp.concatenate([grad_query, key_high, value_high, key_low, value_low], 1)
    grad_norm = nn(terms, back_ref[...])
    weight_terms = nn(normed.T, terms)
    add_qkv = weight_terms[:, : 3 * features] + jnp.concatenate(
        [jnp.zeros((features, features), F32), weight_terms[:, 3 * features :]], 1
    )
    add_proj = nn(attended_t, cot)
    add_gain = jnp.sum(grad_norm * scaled, 0, keepdims=True)

    @pl.when(step == 0)
    def _():
        acc_qkv_ref[...] = add_qkv
        acc_proj_ref[...] = add_proj
        acc_gain_ref[...] = add_gain

    @pl.when(step > 0)
    def _():
        acc_qkv_ref[...] += add_qkv
        acc_proj_ref[...] += add_proj
        acc_gain_ref[...] += add_gain

    grad_hat = grad_norm * gain
    res_ref[...] = cot_ref[...] + inv_std * (
        grad_hat
        - jnp.mean(grad_hat, -1, keepdims=True)
        - scaled * jnp.mean(grad_hat * scaled, -1, keepdims=True)
    )
    for i in range(W):
        for j in range(W):
            at_x, at_y = place(i, j)
            grad_ref[at_x, at_y] = res_ref[pl.ds((i * W + j) * W, W), :].astype(BF16)


def windows_back(offsets, data, norm_gain, qkv_weight, proj_weight):
    extent_x, _, extent_y, _, features = data.shape
    steps = (extent_x // W) * (extent_y // W)
    weight_t = qkv_weight.T
    back = jnp.concatenate([weight_t, weight_t[features:]], 0)
    lanes = jnp.arange(features) // (features // H)
    mask = (lanes[None, :] == jnp.arange(H)[:, None]).astype(BF16)
    whole = pl.BlockSpec(memory_space=pltpu.VMEM)
    rows = W * W * W
    return pl.pallas_call(
        window_kernel,
        grid=(steps,),
        in_specs=[pl.BlockSpec(memory_space=pltpu.SMEM)] + [whole] * 6,
        out_specs=[whole] * 4,
        out_shape=[
            jax.ShapeDtypeStruct((extent_x, extent_y, W, features), BF16),
            jax.ShapeDtypeStruct((features, 3 * features), F32),
            jax.ShapeDtypeStruct((features, features), F32),
            jax.ShapeDtypeStruct((1, features), F32),
        ],
        scratch_shapes=[pltpu.VMEM((rows, features), F32)] * 3,
        compiler_params=pltpu.CompilerParams(vmem_limit_bytes=48 * 1024 * 1024),
        cost_estimate=pl.CostEstimate(
            flops=steps * 12 * rows * rows * features,
            bytes_accessed=3 * data.size,
            transcendentals=steps * H * rows * rows,
        ),
    )(offsets, data, norm_gain.reshape(1, -1), qkv_weight, back, proj_weight.T, mask)


def shift_rows(field, offset, sign):
    count = lax.axis_size("gx")
    for bit_pos in range(3):
        by = sign * (1 << bit_pos)
        moved = lax.ppermute(field, "gx", [(i, (i + by) % count) for i in range(count)])
        field = jnp.where(offset >> bit_pos & 1 == 1, moved, field)
    return field


def exchange(pieces, group):
    count = lax.axis_size("gx")
    groups = None
    if count != group:
        groups = [list(range(i, i + group)) for i in range(0, count, group)]
    return lax.all_to_all(pieces, "gx", 0, 0, axis_index_groups=groups, tiled=True)


def per_device(tokens, cotangent, offsets, norm_gain, qkv_weight, proj_weight):
    _, extent_y, extent_z, features = tokens.shape
    count = lax.axis_size("gx")
    group = extent_z // W
    offset_x = offsets[0]
    stacked = jnp.concatenate([tokens, cotangent], 0)
    if count != group:
        stacked = shift_rows(stacked, offset_x, -1)
        offsets = offsets * jnp.array([0, 1, 1], offsets.dtype)
    stacked = jnp.roll(stacked, -offsets[2], axis=2)
    pieces = stacked.reshape(2, extent_y, group, W, features).transpose(2, 0, 1, 3, 4)
    data = exchange(pieces, group)
    grads, acc_qkv, acc_proj, acc_gain = windows_back(
        offsets, data, norm_gain, qkv_weight, proj_weight
    )
    back = exchange(grads, group)
    field = back.transpose(1, 0, 2, 3).reshape(1, extent_y, extent_z, features)
    field = jnp.roll(field, offsets[2], axis=2)
    if count != group:
        field = shift_rows(field, offset_x, 1)
    summed = lax.psum((acc_qkv, acc_proj, acc_gain[0]), "gx")
    norm_scale = (count * extent_y * extent_z) ** (-0.5)
    return (field, summed[0] * norm_scale, summed[1] * norm_scale, summed[2] * norm_scale)


def solution(mesh):
    rows = P(("rve", "gx"), None, None, None)
    return jax.shard_map(
        per_device,
        mesh=mesh,
        in_specs=(rows, rows, P(), P(), P(), P()),
        out_specs=(rows, P("rve", None), P("rve", None), P("rve")),
        check_vma=False,
    )
```

time: 671 us -> 182 us (0.27)
  matrix products: 251 us -> 0 us
  waiting for transfers between devices: 214 us -> 81.7 us
  local copies, waits for them, and re-layouts: 63.7 us -> 1.62 us
  other arithmetic: 44.7 us -> 7.8 us
  Pallas kernels: 0 us -> 24.9 us
  starting transfers between devices: 38.2 us -> 14.2 us
    dot_general x52 -> x0, matrix products: 234 us -> none  [the longest x4 75 us: attend_back(): jnp.einsum('whqk,wqhd->wkhd', grad_score, query_heads, preferred_element_...]
    ppermute x30 -> x0, waiting for transfers between devices: 151 us -> none  [the longest x24 94.7 us: swapped(): lax.ppermute(value, axis, [(i, i ^ 1 << bit) for i in range(lax.axis_size...]
    ppermute x30 -> x0, starting transfers between devices: 38.2 us -> none  [the longest x24 27.4 us: swapped(): lax.ppermute(value, axis, [(i, i ^ 1 << bit) for i in range(lax.axis_size...]
    reshape x21 -> x1, local copies, waits for them, and re-layouts: 26.8 us -> 0.13 us  [per_device(): field = back.transpose(1, 0, 2, 3).reshape(1, extent_y, extent_z, features)]
    pallas_call x0 -> x1, Pallas kernels: none -> 24.9 us  [windows_back(): pl.pallas_call(window_kernel, grid=(steps,), in_specs=[pl.BlockSpec(memor...]
    all_to_all x0 -> x2, waiting for transfers between devices: none -> 22.8 us  [exchange(): lax.all_to_all(pieces, 'gx', 0, 0, axis_index_groups=groups, tiled=True)]
    convert_element_type x28 -> x1, other arithmetic: 22.3 us -> 0.01 us  [windows_back(): mask = (lanes[None, :] == jnp.arange(H)[:, None]).astype(BF16)]
    slice x25 -> x2, local copies, waits for them, and re-layouts: 22.3 us -> 1.24 us  [the longest x1 1.24 us: per_device(): stacked = jnp.roll(stacked, -offsets[2], axis=2)]
  transfers between devices with their start and end apart: 31 -> 3, of which waited for: 29 -> 2; matrix products, arithmetic and copies ran while one was open for 9% -> 2% of each run, Pallas kernels for 0% -> 0%
where the time goes in v1:
time: 182 us; the launch traced here: 181 us
  waiting for transfers between devices  81.7 us (45%)
  blocking collectives  34.5 us (19%)
  Pallas kernels  24.9 us (14%)
  between operations  16.7 us (9%)
  starting transfers between devices  14.2 us (8%)
  other arithmetic  7.8 us (4%)
    psum x1, waiting for transfers between devices, per_device(): summed = lax.psum((acc_qkv, acc_proj, acc_gain[0]), 'gx')  58.8 us
    psum x1, blocking collectives, per_device(): summed = lax.psum((acc_qkv, acc_proj, acc_gain[0]), 'gx')  34.5 us
    pallas_call x1, Pallas kernels, windows_back(): pl.pallas_call(window_kernel, grid=(steps,), in_specs=[pl.BlockSpec(memor...  24.9 us
    all_to_all x2, waiting for transfers between devices, exchange(): lax.all_to_all(pieces, 'gx', 0, 0, axis_index_groups=groups, tiled=True)  22.8 us
    all_to_all x2, starting transfers between devices, exchange(): lax.all_to_all(pieces, 'gx', 0, 0, axis_index_groups=groups, tiled=True)  14.2 us
  transfers between devices with their start and end apart: 3, of which 2 were waited for; matrix products, arithmetic and copies ran while one was open for 2% of the time, Pallas kernels for 0%

profile of v1, /device:TPU:1, one launch (start us, length us, event | category | flops | bytes accessed | tf_op | source)
XLA Modules:
  0.0 181.4 jit_solution(18306165577430082100)
XLA Ops:
  7.2 1.2 slice.7
  9.7 3.0 %copy_bitcast_fusion = bf16[16,2,16,8,128]{4,3,2,1,0:T(8,128)(2,1)} fusion(s32[]{:T(128)S(6)} %select_n.33, bf16[1,16,128,128]{3,2,1,0:T(8,128)(2,1)} %param.6, bf16[1,16,128,128]{3,2,1,0:T(8,128)(2,1)} %param.7), kind=kLoop, calls=%fused_computation.10 | loop fusion | flops 4194304 | bytes 2097156 | tf_op jit(solution)/shard_map/transpose | solution.py:184
  12.7 0.0 copy-start
  12.7 0.0 copy-start.3
  12.7 7.5 %all-to-all-start = ((bf16[16,2,16,8,128]{4,3,2,1,0:T(8,128)(2,1)}), bf16[16,2,16,8,128]{4,3,2,1,0:T(8,128)(2,1)S(1)}, u32[]{:S(2)}, u32[]{:S(2)}) async-start(bf16[16,2,16,8,128]{4,3,2,1,0:T(8,128)(2,1)} %copy_bitcast_fusion), calls=%async_computation | async-start | bytes 2097152 | tf_op jit(solution)/shard_map/all_to_all | solution.py:171
  20.2 0.0 copy-done
  20.2 0.1 copy.13
  20.4 0.0 copy-done.3
  20.4 0.1 copy.14
  20.5 22.8 %all-to-all-done.data_ref = bf16[16,2,16,8,128]{4,3,2,1,0:T(8,128)(2,1)S(1)} async-done(((bf16[16,2,16,8,128]{4,3,2,1,0:T(8,128)(2,1)}), bf16[16,2,16,8,128]{4,3,2,1,0:T(8,128)(2,1)S(1)}, u32[]{:S(2)}, u32[]{:S(2)}) %all-to-all-start) | async-done | bytes 1048608 | tf_op jit(solution)/shard_map/all_to_all | solution.py:171
  43.4 0.0 copy-done.1
  43.4 0.0 copy-done.2
  43.4 24.9 %shard_map.93 = (bf16[16,16,8,128]{3,2,1,0:T(8,128)(2,1)}, f32[128,384]{1,0:T(8,128)}, f32[128,128]{1,0:T(8,128)}, f32[1,128]{1,0:T(1,128)S(1)}) custom-call(s32[3]{0:T(128)S(1)} %copy-done.1, bf16[16,2,16,8,128]{4,3,2,1,0:T(8,128)(2,1)S(1)} %all-to-all-done.data_ref, f32[1,128]{1,0:T(1,128)S(1)} %bitcast.16, bf16[128,384]{1,0:T(8,128)(2,1)S(1)} %copy-done, ...), custom_call_target="tpu_custom_call" | custom-call | flops 1610612736 | bytes 1572864 | tf_op jit(solution)/shard_map/pallas_call | solution.py:136
  68.2 6.7 %all-to-all-start.1 = ((bf16[16,16,8,128]{3,2,1,0:T(8,128)(2,1)}), bf16[16,16,8,128]{3,2,1,0:T(8,128)(2,1)S(1)}, u32[]{:S(2)}, u32[]{:S(2)}) async-start(bf16[16,16,8,128]{3,2,1,0:T(8,128)(2,1)} %get-tuple-element.8), calls=%async_computation.1 | async-start | bytes 1048576 | tf_op jit(solution)/shard_map/all_to_all | solution.py:171
  74.9 0.0 all-reduce.3.cloned.1.call-start
  76.3 0.0 all-reduce.3.cloned.1.call-update
  76.3 34.5 %psum.23 = f32[128]{0:T(128)S(1)} all-reduce(f32[128]{0:T(128)S(1)} %bitcast.17), channel_id=1, replica_groups=mesh['rve'=2,'gx'=16] {'gx'}, use_global_device_ids=true, to_apply=%region_2.3 | all-reduce | flops 128 | bytes 1024 | tf_op jit(solution)/shard_map/psum | solution.py:194
  110.8 0.5 broadcast_multiply_fusion.2
  111.3 58.8 %all-reduce.3.cloned.1.call-done = (f32[128,384]{1,0:T(8,128)}, f32[128,128]{1,0:T(8,128)}) async-done(((f32[128,384]{1,0:T(8,128)}, f32[128,128]{1,0:T(8,128)}), (f32[128,384]{1,0:T(8,128)}, f32[128,128]{1,0:T(8,128)})) %all-reduce.3.cloned.1.call-update) | async-done | bytes 262160 | tf_op jit(solution)/shard_map/psum | solution.py:194
  170.2 1.5 broadcast_multiply_fusion.1
  171.6 1.6 broadcast_multiply_fusion
  173.3 0.0 all-to-all-done.1
  173.3 0.1 copy_bitcast_fusion.1
  173.4 1.2 fusion.4
  (6 shorter events, 0.0 us)
Async XLA Ops:
  12.7 7.5 %copy-start = (bf16[128,384]{1,0:T(8,128)(2,1)S(1)}, bf16[128,384]{1,0:T(8,128)(2,1)}, u32[]{:S(2)}) copy-start(bf16[128,384]{1,0:T(8,128)(2,1)} %qkv_ref.1) | copy-start | bytes 294916
  12.7 7.7 %copy-start.3 = (bf16[128,128]{1,0:T(8,128)(2,1)S(1)}, bf16[128,128]{1,0:T(8,128)(2,1)}, u32[]{:S(2)}) copy-start(bf16[128,128]{1,0:T(8,128)(2,1)} %param.11) | copy-start | bytes 98308
  12.7 30.6 %copy-start.1 = (s32[3]{0:T(128)S(1)}, s32[3]{0:T(128)}, u32[]{:S(2)}) copy-start(s32[3]{0:T(128)} %offsets_ref.1) | copy-start | bytes 40
  12.7 30.6 %copy-start.2 = (f32[128]{0:T(128)S(1)}, f32[128]{0:T(128)}, u32[]{:S(2)}) copy-start(f32[128]{0:T(128)} %param.9) | copy-start | bytes 1540
  12.7 30.6 %all-to-all-start = ((bf16[16,2,16,8,128]{4,3,2,1,0:T(8,128)(2,1)}), bf16[16,2,16,8,128]{4,3,2,1,0:T(8,128)(2,1)S(1)}, u32[]{:S(2)}, u32[]{:S(2)}) async-start(bf16[16,2,16,8,128]{4,3,2,1,0:T(8,128)(2,1)} %copy_bitcast_fusion), calls=%async_computation | async-start | bytes 2097152 | tf_op jit(solution)/shard_map/all_to_all | solution.py:171
  68.2 105.0 %all-to-all-start.1 = ((bf16[16,16,8,128]{3,2,1,0:T(8,128)(2,1)}), bf16[16,16,8,128]{3,2,1,0:T(8,128)(2,1)S(1)}, u32[]{:S(2)}, u32[]{:S(2)}) async-start(bf16[16,16,8,128]{3,2,1,0:T(8,128)(2,1)} %get-tuple-element.8), calls=%async_computation.1 | async-start | bytes 1048576 | tf_op jit(solution)/shard_map/all_to_all | solution.py:171
  74.9 95.3 %all-reduce.3.cloned.1.call-start = ((), (), s32[]{:S(2)}) async-start(), calls=%async_computation.2 | async-start | bytes 524288 | tf_op jit(solution)/shard_map/psum | solution.py:194
Sparse Core Ops, SparseCore 0:
  79.7 90.3 all-reduce.2

commit v2 on v1

--- a/solution.py
+++ b/solution.py
@@ -28,7 +28,7 @@
 
 def window_kernel(
     offsets_ref, data_ref, gain_ref, qkv_ref, back_ref, proj_t_ref, mask_ref,
-    grad_ref, acc_qkv_ref, acc_proj_ref, acc_gain_ref,
+    grad_ref, acc_ref,
     tok_ref, cot_ref, res_ref,
 ):
     extent_x, _, extent_y = data_ref.shape[:3]
@@ -102,15 +102,11 @@
 
     @pl.when(step == 0)
     def _():
-        acc_qkv_ref[...] = add_qkv
-        acc_proj_ref[...] = add_proj
-        acc_gain_ref[...] = add_gain
-
-    @pl.when(step > 0)
-    def _():
-        acc_qkv_ref[...] += add_qkv
-        acc_proj_ref[...] += add_proj
-        acc_gain_ref[...] += add_gain
+        acc_ref[...] = jnp.zeros_like(acc_ref)
+
+    acc_ref[:, : 3 * features] += add_qkv
+    acc_ref[:, 3 * features : 4 * features] += add_proj
+    acc_ref[0:1, 4 * features :] += add_gain
 
     grad_hat = grad_norm * gain
     res_ref[...] = cot_ref[...] + inv_std * (
@@ -137,12 +133,10 @@
         window_kernel,
         grid=(steps,),
         in_specs=[pl.BlockSpec(memory_space=pltpu.SMEM)] + [whole] * 6,
-        out_specs=[whole] * 4,
+        out_specs=[whole] * 2,
         out_shape=[
             jax.ShapeDtypeStruct((extent_x, extent_y, W, features), BF16),
-            jax.ShapeDtypeStruct((features, 3 * features), F32),
-            jax.ShapeDtypeStruct((features, features), F32),
-            jax.ShapeDtypeStruct((1, features), F32),
+            jax.ShapeDtypeStruct((features, 5 * features), F32),
         ],
         scratch_shapes=[pltpu.VMEM((rows, features), F32)] * 3,
         compiler_params=pltpu.CompilerParams(vmem_limit_bytes=48 * 1024 * 1024),
@@ -152,6 +146,80 @@
             transcendentals=steps * H * rows * rows,
         ),
     )(offsets, data, norm_gain.reshape(1, -1), qkv_weight, back, proj_weight.T, mask)
+
+
+def return_kernel(
+    group, grads_ref, acc_ref, field_ref, total_ref,
+    slots, part, acc_send, acc_recv, all_send, all_recv, grad_send, grad_recv,
+):
+    me = lax.axis_index("gx")
+    mine = lax.rem(me, group)
+    base = me - mine
+    others = [lax.rem(mine + r, group) for r in range(1, group)]
+
+    barrier = pltpu.get_barrier_semaphore()
+    for other in others:
+        pl.semaphore_signal(
+            barrier, inc=1, device_id={"gx": base + other}, device_id_type=pl.DeviceIdType.MESH
+        )
+    pl.semaphore_wait(barrier, group - 1)
+
+    def copies(source, target, send, recv):
+        out = []
+        for at, other in enumerate(others):
+            copy = pltpu.make_async_remote_copy(
+                src_ref=source(other),
+                dst_ref=target(at),
+                send_sem=send.at[at],
+                recv_sem=recv.at[at],
+                device_id={"gx": base + other},
+                device_id_type=pl.DeviceIdType.MESH,
+            )
+            copy.start()
+            out.append(copy)
+        return out
+
+    terms = copies(lambda p: acc_ref.at[p], lambda at: slots.at[at], acc_send, acc_recv)
+    rows = copies(lambda p: grads_ref.at[p], lambda at: field_ref.at[mine], grad_send, grad_recv)
+    field_ref[mine] = grads_ref[mine]
+    summed = acc_ref[mine]
+    for at, copy in enumerate(terms):
+        copy.wait_recv()
+        summed = summed + slots[at]
+    part[...] = summed
+    sums = copies(lambda p: part, lambda at: total_ref.at[mine], all_send, all_recv)
+    total_ref[mine] = summed
+    for copy in rows + sums:
+        copy.wait_recv()
+    for copy in terms + rows + sums:
+        copy.wait_send()
+
+
+def return_and_sum(grads, acc, group):
+    features = grads.shape[-1]
+    pieces = grads.reshape(group, -1, features)
+    parts = acc.reshape(group, -1, acc.shape[-1])
+    whole = pl.BlockSpec(memory_space=pltpu.VMEM)
+    sems = pltpu.SemaphoreType.DMA((group - 1,))
+    field, total = pl.pallas_call(
+        lambda *refs: return_kernel(group, *refs),
+        in_specs=[whole] * 2,
+        out_specs=[whole] * 2,
+        out_shape=[
+            jax.ShapeDtypeStruct(pieces.shape, pieces.dtype),
+            jax.ShapeDtypeStruct(parts.shape, parts.dtype),
+        ],
+        scratch_shapes=[
+            pltpu.VMEM((group - 1,) + parts.shape[1:], F32),
+            pltpu.VMEM(parts.shape[1:], F32),
+        ]
+        + [sems] * 6,
+        compiler_params=pltpu.CompilerParams(
+            collective_id=0, has_side_effects=True, vmem_limit_bytes=32 * 1024 * 1024
+        ),
+        name="return_and_sum",
+    )(pieces, parts)
+    return field.reshape(grads.shape), total.reshape(acc.shape)
 
 
 def shift_rows(field, offset, sign):
@@ -183,17 +251,20 @@
     stacked = jnp.roll(stacked, -offsets[2], axis=2)
     pieces = stacked.reshape(2, extent_y, group, W, features).transpose(2, 0, 1, 3, 4)
     data = exchange(pieces, group)
-    grads, acc_qkv, acc_proj, acc_gain = windows_back(
-        offsets, data, norm_gain, qkv_weight, proj_weight
-    )
-    back = exchange(grads, group)
+    grads, acc = windows_back(offsets, data, norm_gain, qkv_weight, proj_weight)
+    back, total = return_and_sum(grads, acc, group)
     field = back.transpose(1, 0, 2, 3).reshape(1, extent_y, extent_z, features)
     field = jnp.roll(field, offsets[2], axis=2)
     if count != group:
         field = shift_rows(field, offset_x, 1)
-    summed = lax.psum((acc_qkv, acc_proj, acc_gain[0]), "gx")
-    norm_scale = (count * extent_y * extent_z) ** (-0.5)
-    return (field, summed[0] * norm_scale, summed[1] * norm_scale, summed[2] * norm_scale)
+        total = lax.psum(total * (1.0 / group), "gx")
+    total = total * (count * extent_y * extent_z) ** (-0.5)
+    return (
+        field,
+        total[:, : 3 * features],
+        total[:, 3 * features : 4 * features],
+        total[0, 4 * features :],
+    )
 
 
 def solution(mesh):

time: 182 us -> 95.4 us (0.52)
  waiting for transfers between devices: 81.7 us -> 21.5 us
  blocking collectives: 34.5 us -> 0 us
  Pallas kernels: 24.9 us -> 54.9 us
  between operations: 16.7 us -> 3.36 us
  starting transfers between devices: 14.2 us -> 7.49 us
  other arithmetic: 7.8 us -> 4.22 us
  local copies, waits for them, and re-layouts: 1.62 us -> 3.45 us
    psum x1 -> x0, waiting for transfers between devices: 58.8 us -> none  [per_device(): summed = lax.psum((acc_qkv, acc_proj, acc_gain[0]), 'gx')]
    psum x1 -> x0, blocking collectives: 34.5 us -> none  [per_device(): summed = lax.psum((acc_qkv, acc_proj, acc_gain[0]), 'gx')]
    pallas_call x0 -> x1, Pallas kernels: none -> 30.9 us  [return_and_sum(): pl.pallas_call(lambda *refs: return_kernel(group, *refs), in_specs=[whole...]
    all_to_all x2 -> x1, starting transfers between devices: 14.2 us -> 7.49 us  [exchange(): lax.all_to_all(pieces, 'gx', 0, 0, axis_index_groups=groups, tiled=True)]
    mul x3 -> x1, other arithmetic: 3.61 us -> 0.03 us  [per_device(): total = total * (count * extent_y * extent_z) ** (-0.5)]
    all_to_all x2 -> x1, waiting for transfers between devices: 22.8 us -> 21.5 us  [exchange(): lax.all_to_all(pieces, 'gx', 0, 0, axis_index_groups=groups, tiled=True)]
  transfers between devices with their start and end apart: 3 -> 1, of which waited for: 2 -> 1; matrix products, arithmetic and copies ran while one was open for 2% -> 0% of each run, Pallas kernels for 0% -> 0%
where the time goes in v2:
time: 95.4 us; the launch traced here: 95 us
  Pallas kernels  54.9 us (58%)
  waiting for transfers between devices  21.5 us (23%)
  starting transfers between devices  7.49 us (8%)
  other arithmetic  4.22 us (4%)
  local copies, waits for them, and re-layouts  3.45 us (4%)
  between operations  3.36 us (4%)
    pallas_call x1, Pallas kernels, return_and_sum(): pl.pallas_call(lambda *refs: return_kernel(group, *refs), in_specs=[whole...  30.9 us
    pallas_call x1, Pallas kernels, windows_back(): pl.pallas_call(window_kernel, grid=(steps,), in_specs=[pl.BlockSpec(memor...  24.1 us
    all_to_all x1, waiting for transfers between devices, exchange(): lax.all_to_all(pieces, 'gx', 0, 0, axis_index_groups=groups, tiled=True)  21.5 us
    all_to_all x1, starting transfers between devices, exchange(): lax.all_to_all(pieces, 'gx', 0, 0, axis_index_groups=groups, tiled=True)  7.49 us
    transpose x1, other arithmetic, per_device(): stacked.reshape(2, extent_y, group, W, features).transpose(2, 0, 1, 3, 4)  3 us
  transfers between devices with their start and end apart: 1, of which 1 were waited for; matrix products, arithmetic and copies ran while one was open for 0% of the time, Pallas kernels for 0%

profile of v2, /device:TPU:1, one launch (start us, length us, event | category | flops | bytes accessed | tf_op | source)
XLA Modules:
  0.0 95.0 jit_solution(3586120278578664836)
XLA Ops:
  0.6 1.2 %slice.16 = s32[1]{0:T(128)} slice(s32[3]{0:T(128)} %offsets_ref.1), slice={[2:3]} | slice | bytes 8 | tf_op jit(solution)/shard_map/slice | solution.py:251
  3.2 3.0 %copy_bitcast_fusion = bf16[16,2,16,8,128]{4,3,2,1,0:T(8,128)(2,1)} fusion(s32[]{:T(128)S(6)} %select_n.33, bf16[1,16,128,128]{3,2,1,0:T(8,128)(2,1)} %param.6, bf16[1,16,128,128]{3,2,1,0:T(8,128)(2,1)} %param.7), kind=kLoop, calls=%fused_computation.10 | loop fusion | flops 4194304 | bytes 2097156 | tf_op jit(solution)/shard_map/transpose | solution.py:252
  6.2 0.0 copy-start
  6.2 0.0 copy-start.3
  6.2 0.0 copy-start.1
  6.2 0.0 copy-start.2
  6.2 7.5 %all-to-all-start = ((bf16[16,2,16,8,128]{4,3,2,1,0:T(8,128)(2,1)}), bf16[16,2,16,8,128]{4,3,2,1,0:T(8,128)(2,1)S(1)}, u32[]{:S(2)}, u32[]{:S(2)}) async-start(bf16[16,2,16,8,128]{4,3,2,1,0:T(8,128)(2,1)} %copy_bitcast_fusion), calls=%async_computation | async-start | bytes 2097152 | tf_op jit(solution)/shard_map/all_to_all | solution.py:239
  15.0 0.0 copy-done
  15.0 0.1 copy.14
  15.2 0.0 copy-done.3
  15.2 0.1 copy.15
  15.3 21.5 %all-to-all-done.data_ref = bf16[16,2,16,8,128]{4,3,2,1,0:T(8,128)(2,1)S(1)} async-done(((bf16[16,2,16,8,128]{4,3,2,1,0:T(8,128)(2,1)}), bf16[16,2,16,8,128]{4,3,2,1,0:T(8,128)(2,1)S(1)}, u32[]{:S(2)}, u32[]{:S(2)}) %all-to-all-start) | async-done | bytes 1048608 | tf_op jit(solution)/shard_map/all_to_all | solution.py:239
  36.8 0.0 copy-done.1
  36.8 0.0 copy-done.2
  36.8 24.1 %shard_map.93 = (bf16[16,16,8,128]{3,2,1,0:T(8,128)(2,1)S(1)}, f32[128,640]{1,0:T(8,128)S(1)}) custom-call(s32[3]{0:T(128)S(1)} %copy-done.1, bf16[16,2,16,8,128]{4,3,2,1,0:T(8,128)(2,1)S(1)} %all-to-all-done.data_ref, f32[1,128]{1,0:T(1,128)S(1)} %bitcast.25, bf16[128,384]{1,0:T(8,128)(2,1)S(1)} %copy-done, bf16[640,128]{1,0:T(8,128)(2,1)S(1)} %pad_maximum_fusion.back_ref, ...), custom_call_target="tpu_custom_call" | custom-call | flops 1610612736 | bytes 1572864 | tf_op jit(solution)/shard_map/pallas_call | solution.py:132
  60.9 30.9 %return_and_sum.1 = (bf16[16,128,128]{2,1,0:T(8,128)(2,1)S(1)}, f32[16,8,640]{2,1,0:T(8,128)S(1)}) custom-call(bf16[16,128,128]{2,1,0:T(8,128)(2,1)S(1)} %bitcast.22, f32[16,8,640]{2,1,0:T(8,128)S(1)} %bitcast.23), custom_call_target="tpu_custom_call" | custom-call | tf_op jit(solution)/shard_map/return_and_sum/pallas_call | solution.py:204
  91.8 0.7 slice.22
  92.5 0.6 slice.23
  93.1 0.5 slice_bitcast_fusion
  93.7 0.1 copy_bitcast_fusion.1
  93.8 1.2 %fusion.4 = bf16[1,16,128,128]{3,2,1,0:T(8,128)(2,1)} fusion(s32[]{:T(128)S(6)} %select_n.36, bf16[1,16,128,128]{3,2,1,0:T(8,128)(2,1)S(1)} %copy_bitcast_fusion.1), kind=kLoop, calls=%fused_computation.11 | loop fusion | flops 1048576 | bytes 1048580 | tf_op jit(solution)/shard_map/jit(_roll_dynamic)/concatenate | solution.py:257
  (5 shorter events, 0.1 us)
Async XLA Ops:
  6.2 8.8 %copy-start = (bf16[128,384]{1,0:T(8,128)(2,1)S(1)}, bf16[128,384]{1,0:T(8,128)(2,1)}, u32[]{:S(2)}) copy-start(bf16[128,384]{1,0:T(8,128)(2,1)} %qkv_ref.1) | copy-start | bytes 294916
  6.2 9.0 %copy-start.3 = (bf16[128,128]{1,0:T(8,128)(2,1)S(1)}, bf16[128,128]{1,0:T(8,128)(2,1)}, u32[]{:S(2)}) copy-start(bf16[128,128]{1,0:T(8,128)(2,1)} %param.11) | copy-start | bytes 98308
  6.2 30.6 %copy-start.1 = (s32[3]{0:T(128)S(1)}, s32[3]{0:T(128)}, u32[]{:S(2)}) copy-start(s32[3]{0:T(128)} %offsets_ref.1) | copy-start | bytes 40
  6.2 30.6 %copy-start.2 = (f32[128]{0:T(128)S(1)}, f32[128]{0:T(128)}, u32[]{:S(2)}) copy-start(f32[128]{0:T(128)} %param.9) | copy-start | bytes 1540
  6.2 30.6 %all-to-all-start = ((bf16[16,2,16,8,128]{4,3,2,1,0:T(8,128)(2,1)}), bf16[16,2,16,8,128]{4,3,2,1,0:T(8,128)(2,1)S(1)}, u32[]{:S(2)}, u32[]{:S(2)}) async-start(bf16[16,2,16,8,128]{4,3,2,1,0:T(8,128)(2,1)} %copy_bitcast_fusion), calls=%async_computation | async-start | bytes 2097152 | tf_op jit(solution)/shard_map/all_to_all | solution.py:239

commit v3 on v2

--- a/solution.py
+++ b/solution.py
@@ -27,7 +27,7 @@
 
 
 def window_kernel(
-    offsets_ref, data_ref, gain_ref, qkv_ref, back_ref, proj_t_ref, mask_ref,
+    offsets_ref, data_ref, gain_ref, qkv_ref, back_ref, proj_t_ref, mask_ref, start_ref,
     grad_ref, acc_ref,
     tok_ref, cot_ref, res_ref,
 ):
@@ -36,10 +36,10 @@
     step = pl.program_id(0)
     per_y = extent_y // W
     first_x = (step // per_y) * W + offsets_ref[0]
-    first_y = (step % per_y) * W + offsets_ref[1]
+    first_y = (step % per_y) * W
 
     def place(i, j):
-        return lax.rem(first_x + i, extent_x), lax.rem(first_y + j, extent_y)
+        return lax.rem(first_x + i, extent_x), first_y + j
 
     for i in range(W):
         for j in range(W):
@@ -102,7 +102,7 @@
 
     @pl.when(step == 0)
     def _():
-        acc_ref[...] = jnp.zeros_like(acc_ref)
+        acc_ref[...] = start_ref[...]
 
     acc_ref[:, : 3 * features] += add_qkv
     acc_ref[:, 3 * features : 4 * features] += add_proj
@@ -120,7 +120,7 @@
             grad_ref[at_x, at_y] = res_ref[pl.ds((i * W + j) * W, W), :].astype(BF16)
 
 
-def windows_back(offsets, data, norm_gain, qkv_weight, proj_weight):
+def windows_back(offsets, data, norm_gain, qkv_weight, proj_weight, start):
     extent_x, _, extent_y, _, features = data.shape
     steps = (extent_x // W) * (extent_y // W)
     weight_t = qkv_weight.T
@@ -132,7 +132,7 @@
     return pl.pallas_call(
         window_kernel,
         grid=(steps,),
-        in_specs=[pl.BlockSpec(memory_space=pltpu.SMEM)] + [whole] * 6,
+        in_specs=[pl.BlockSpec(memory_space=pltpu.SMEM)] + [whole] * 7,
         out_specs=[whole] * 2,
         out_shape=[
             jax.ShapeDtypeStruct((extent_x, extent_y, W, features), BF16),
@@ -145,7 +145,7 @@
             bytes_accessed=3 * data.size,
             transcendentals=steps * H * rows * rows,
         ),
-    )(offsets, data, norm_gain.reshape(1, -1), qkv_weight, back, proj_weight.T, mask)
+    )(offsets, data, norm_gain.reshape(1, -1), qkv_weight, back, proj_weight.T, mask, start)
 
 
 def return_kernel(
@@ -248,13 +248,20 @@
     if count != group:
         stacked = shift_rows(stacked, offset_x, -1)
         offsets = offsets * jnp.array([0, 1, 1], offsets.dtype)
-    stacked = jnp.roll(stacked, -offsets[2], axis=2)
-    pieces = stacked.reshape(2, extent_y, group, W, features).transpose(2, 0, 1, 3, 4)
-    data = exchange(pieces, group)
-    grads, acc = windows_back(offsets, data, norm_gain, qkv_weight, proj_weight)
+    stacked = jnp.roll(stacked, (-offsets[1], -offsets[2]), axis=(1, 2))
+    bands = stacked.reshape(2, extent_y // W, W, group, W, features).transpose(1, 3, 0, 2, 4, 5)
+    arrived = [exchange(band, group) for band in bands]
+    acc = jnp.zeros((features, 5 * features), F32)
+    returned = []
+    for at, data in enumerate(arrived):
+        grads, acc = windows_back(offsets, data, norm_gain, qkv_weight, proj_weight, acc)
+        if at + 1 < len(arrived):
+            returned.append(exchange(grads, group))
     back, total = return_and_sum(grads, acc, group)
-    field = back.transpose(1, 0, 2, 3).reshape(1, extent_y, extent_z, features)
-    field = jnp.roll(field, offsets[2], axis=2)
+    returned.append(back)
+    field = jnp.concatenate(returned, 1).transpose(1, 0, 2, 3)
+    field = field.reshape(1, extent_y, extent_z, features)
+    field = jnp.roll(field, (offsets[1], offsets[2]), axis=(1, 2))
     if count != group:
         field = shift_rows(field, offset_x, 1)
         total = lax.psum(total * (1.0 / group), "gx")

time: 95.4 us -> 97.3 us (1.020)
  waiting for transfers between devices: 21.5 us -> 0.01 us
  blocking collectives: 0 us -> 21.3 us
  Pallas kernels: 54.9 us -> 50.1 us
  starting transfers between devices: 7.49 us -> 10.6 us
  between operations: 3.36 us -> 6.03 us
  local copies, waits for them, and re-layouts: 3.45 us -> 4.6 us
    all_to_all x1 -> x2, waiting for transfers between devices: 21.5 us -> 0.01 us  [exchange(): lax.all_to_all(pieces, 'gx', 0, 0, axis_index_groups=groups, tiled=True)]
    all_to_all x0 -> x1, blocking collectives: none -> 21.3 us  [exchange(): lax.all_to_all(pieces, 'gx', 0, 0, axis_index_groups=groups, tiled=True)]
    pallas_call x1, Pallas kernels: 30.9 us -> 24.8 us  [return_and_sum(): pl.pallas_call(lambda *refs: return_kernel(group, *refs), in_specs=[whole...]
    all_to_all x1 -> x2, starting transfers between devices: 7.49 us -> 10.6 us  [exchange(): lax.all_to_all(pieces, 'gx', 0, 0, axis_index_groups=groups, tiled=True)]
    transpose x1 -> x0, other arithmetic: 3 us -> none  [per_device(): stacked.reshape(2, extent_y, group, W, features).transpose(2, 0, 1, 3, 4)]
    concatenate x1 -> x4, other arithmetic: 1.17 us -> 3.92 us  [the longest x2 2.54 us: per_device(): stacked = jnp.roll(stacked, (-offsets[1], -offsets[2]), axis=(1, 2))]
    pallas_call x1 -> x2, Pallas kernels: 24.1 us -> 25.3 us  [windows_back(): pl.pallas_call(window_kernel, grid=(steps,), in_specs=[pl.BlockSpec(memor...]
  transfers between devices with their start and end apart: 1 -> 2, of which waited for: 1 -> 0; matrix products, arithmetic and copies ran while one was open for 0% -> 2% of each run, Pallas kernels for 0% -> 52%
where the time goes in v3:
time: 97.3 us; the launch traced here: 96.9 us
  Pallas kernels  50.1 us (51%)
  blocking collectives  21.3 us (22%)
  starting transfers between devices  10.6 us (11%)
  between operations  6.03 us (6%)
  local copies, waits for them, and re-layouts  4.6 us (5%)
  other arithmetic  4.1 us (4%)
    pallas_call x2, Pallas kernels, windows_back(): pl.pallas_call(window_kernel, grid=(steps,), in_specs=[pl.BlockSpec(memor...  25.3 us
    pallas_call x1, Pallas kernels, return_and_sum(): pl.pallas_call(lambda *refs: return_kernel(group, *refs), in_specs=[whole...  24.8 us
    all_to_all x1, blocking collectives, exchange(): lax.all_to_all(pieces, 'gx', 0, 0, axis_index_groups=groups, tiled=True)  21.3 us
    all_to_all x2, starting transfers between devices, exchange(): lax.all_to_all(pieces, 'gx', 0, 0, axis_index_groups=groups, tiled=True)  10.6 us
    concatenate x2, other arithmetic, per_device(): stacked = jnp.roll(stacked, (-offsets[1], -offsets[2]), axis=(1, 2))  2.54 us
  transfers between devices with their start and end apart: 2, of which 0 were waited for; matrix products, arithmetic and copies ran while one was open for 2% of the time, Pallas kernels for 52%

profile of v3, /device:TPU:1, one launch (start us, length us, event | category | flops | bytes accessed | tf_op | source)
XLA Modules:
  0.0 96.9 jit_solution(10878854340093871955)
XLA Ops:
  0.6 1.3 %fusion.7 = (s32[1]{0:T(128)}, s32[1]{0:T(128)}) fusion(s32[3]{0:T(128)} %offsets_ref.3), kind=kLoop, calls=%fused_computation.30 | loop fusion | bytes 16 | tf_op jit(solution)/shard_map/slice | solution.py:251
  4.6 1.8 %fusion.2 = bf16[2,16,128,128]{3,2,1,0:T(8,128)(2,1)S(1)} fusion(s32[]{:T(128)S(6)} %select_n.56, bf16[1,16,128,128]{3,2,1,0:T(8,128)(2,1)} %param.6, bf16[1,16,128,128]{3,2,1,0:T(8,128)(2,1)} %param.7), kind=kLoop, calls=%fused_computation.8 | loop fusion | flops 1572864 | bytes 2097156 | tf_op jit(solution)/shard_map/jit(_roll_dynamic)/concatenate | solution.py:251
  6.3 0.8 fusion
  7.1 0.3 copy.18
  7.4 0.9 slice_bitcast_fusion.1
  8.3 21.3 %all_to_all.15.data_ref = bf16[16,2,8,8,128]{4,3,2,1,0:T(8,128)(2,1)S(1)} all-to-all(bf16[16,2,8,8,128]{4,3,2,1,0:T(8,128)(2,1)S(1)} %get-tuple-element.16), channel_id=1, replica_groups=mesh['rve'=2,'gx'=16] {'gx'}, dimensions={0} | all-to-all | bytes 1048576 | tf_op jit(solution)/shard_map/all_to_all | solution.py:239
  29.6 4.6 %all-to-all-start.2 = ((bf16[16,2,8,8,128]{4,3,2,1,0:T(8,128)(2,1)}), bf16[16,2,8,8,128]{4,3,2,1,0:T(8,128)(2,1)S(1)}, u32[]{:S(2)}, u32[]{:S(2)}) async-start(bf16[16,2,8,8,128]{4,3,2,1,0:T(8,128)(2,1)} %get-tuple-element.17), calls=%async_computation.2 | async-start | bytes 1048576 | tf_op jit(solution)/shard_map/all_to_all | solution.py:239
  36.9 0.0 copy-done
  36.9 0.1 copy.13
  37.0 0.0 copy-done.3
  37.1 0.1 copy.14
  37.3 0.0 copy-done.1
  37.3 13.0 %shard_map.93 = (bf16[16,8,8,128]{3,2,1,0:T(8,128)(2,1)}, f32[128,640]{1,0:T(8,128)S(1)}) custom-call(s32[3]{0:T(128)S(1)} %copy-done.1, bf16[16,2,8,8,128]{4,3,2,1,0:T(8,128)(2,1)S(1)} %all_to_all.15.data_ref, f32[1,128]{1,0:T(1,128)S(1)} %bitcast.30, bf16[128,384]{1,0:T(8,128)(2,1)S(1)} %copy-done, bf16[640,128]{1,0:T(8,128)(2,1)S(1)} %pad_maximum_fusion.back_ref, ...), custom_call_target="tpu_custom_call" | custom-call | flops 805306368 | bytes 786432 | tf_op jit(solution)/shard_map/pallas_call | solution.py:132
  50.3 0.0 all-to-all-done.2.data_ref
  50.3 6.0 %all-to-all-start.1 = ((bf16[16,8,8,128]{3,2,1,0:T(8,128)(2,1)}), bf16[16,8,8,128]{3,2,1,0:T(8,128)(2,1)S(1)}, u32[]{:S(2)}, u32[]{:S(2)}) async-start(bf16[16,8,8,128]{3,2,1,0:T(8,128)(2,1)} %get-tuple-element.10), calls=%async_computation.1 | async-start | bytes 524288 | tf_op jit(solution)/shard_map/all_to_all | solution.py:239
  56.3 12.3 %shard_map.94 = (bf16[16,8,8,128]{3,2,1,0:T(8,128)(2,1)S(1)}, f32[128,640]{1,0:T(8,128)S(1)}) custom-call(s32[3]{0:T(128)S(1)} %copy-done.1, bf16[16,2,8,8,128]{4,3,2,1,0:T(8,128)(2,1)S(1)} %all-to-all-done.2.data_ref, f32[1,128]{1,0:T(1,128)S(1)} %bitcast.31, bf16[128,384]{1,0:T(8,128)(2,1)S(1)} %copy-done, bf16[640,128]{1,0:T(8,128)(2,1)S(1)} %pad_maximum_fusion.back_ref, ...), custom_call_target="tpu_custom_call" | custom-call | flops 805306368 | bytes 786432 | tf_op jit(solution)/shard_map/pallas_call | solution.py:132
  68.6 24.8 %return_and_sum.1 = (bf16[16,64,128]{2,1,0:T(8,128)(2,1)S(1)}, f32[16,8,640]{2,1,0:T(8,128)S(1)}) custom-call(bf16[16,64,128]{2,1,0:T(8,128)(2,1)S(1)} %bitcast.26, f32[16,8,640]{2,1,0:T(8,128)S(1)} %bitcast.25), custom_call_target="tpu_custom_call" | custom-call | tf_op jit(solution)/shard_map/return_and_sum/pallas_call | solution.py:204
  93.5 0.7 slice.28
  94.2 0.6 slice.29
  94.8 0.5 slice_bitcast_fusion.2
  95.3 0.0 all-to-all-done.1
  95.3 0.1 copy_bitcast_fusion.1
  95.5 0.2 fusion.5
  95.7 1.2 %fusion.4 = bf16[1,16,128,128]{3,2,1,0:T(8,128)(2,1)} fusion(s32[]{:T(128)S(6)} %select_n.63, bf16[1,16,128,128]{3,2,1,0:T(8,128)(2,1)S(1)} %fusion.5), kind=kLoop, calls=%fused_computation.15 | loop fusion | flops 1048576 | bytes 1048580 | tf_op jit(solution)/shard_map/jit(_roll_dynamic)/concatenate | solution.py:264
  (11 shorter events, 0.1 us)
Async XLA Ops:
  8.3 28.6 %copy-start = (bf16[128,384]{1,0:T(8,128)(2,1)S(1)}, bf16[128,384]{1,0:T(8,128)(2,1)}, u32[]{:S(2)}) copy-start(bf16[128,384]{1,0:T(8,128)(2,1)} %qkv_ref.3) | copy-start | bytes 294916
  8.3 28.7 %copy-start.3 = (bf16[128,128]{1,0:T(8,128)(2,1)S(1)}, bf16[128,128]{1,0:T(8,128)(2,1)}, u32[]{:S(2)}) copy-start(bf16[128,128]{1,0:T(8,128)(2,1)} %param.11) | copy-start | bytes 98308
  29.6 7.6 %copy-start.1 = (s32[3]{0:T(128)S(1)}, s32[3]{0:T(128)}, u32[]{:S(2)}) copy-start(s32[3]{0:T(128)} %offsets_ref.3) | copy-start | bytes 40
  29.6 7.6 %copy-start.2 = (f32[128]{0:T(128)S(1)}, f32[128]{0:T(128)}, u32[]{:S(2)}) copy-start(f32[128]{0:T(128)} %param.9) | copy-start | bytes 1540
  29.6 20.7 %all-to-all-start.2 = ((bf16[16,2,8,8,128]{4,3,2,1,0:T(8,128)(2,1)}), bf16[16,2,8,8,128]{4,3,2,1,0:T(8,128)(2,1)S(1)}, u32[]{:S(2)}, u32[]{:S(2)}) async-start(bf16[16,2,8,8,128]{4,3,2,1,0:T(8,128)(2,1)} %get-tuple-element.17), calls=%async_computation.2 | async-start | bytes 1048576 | tf_op jit(solution)/shard_map/all_to_all | solution.py:239
  50.3 45.0 %all-to-all-start.1 = ((bf16[16,8,8,128]{3,2,1,0:T(8,128)(2,1)}), bf16[16,8,8,128]{3,2,1,0:T(8,128)(2,1)S(1)}, u32[]{:S(2)}, u32[]{:S(2)}) async-start(bf16[16,8,8,128]{3,2,1,0:T(8,128)(2,1)} %get-tuple-element.10), calls=%async_computation.1 | async-start | bytes 524288 | tf_op jit(solution)/shard_map/all_to_all | solution.py:239

commit v4 on v2

--- a/solution.py
+++ b/solution.py
@@ -222,6 +222,53 @@
     return field.reshape(grads.shape), total.reshape(acc.shape)
 
 
+def spread_kernel(group, pieces_ref, arrived_ref, send, recv):
+    me = lax.axis_index("gx")
+    mine = lax.rem(me, group)
+    base = me - mine
+    others = [lax.rem(mine + r, group) for r in range(1, group)]
+    barrier = pltpu.get_barrier_semaphore()
+    for other in others:
+        pl.semaphore_signal(
+            barrier, inc=1, device_id={"gx": base + other}, device_id_type=pl.DeviceIdType.MESH
+        )
+    pl.semaphore_wait(barrier, group - 1)
+    copies = []
+    for at, other in enumerate(others):
+        copy = pltpu.make_async_remote_copy(
+            src_ref=pieces_ref.at[other],
+            dst_ref=arrived_ref.at[mine],
+            send_sem=send.at[at],
+            recv_sem=recv.at[at],
+            device_id={"gx": base + other},
+            device_id_type=pl.DeviceIdType.MESH,
+        )
+        copy.start()
+        copies.append(copy)
+    arrived_ref[mine] = pieces_ref[mine]
+    for copy in copies:
+        copy.wait_recv()
+    for copy in copies:
+        copy.wait_send()
+
+
+def spread(pieces, group):
+    flat = pieces.reshape(group, -1, pieces.shape[-1])
+    whole = pl.BlockSpec(memory_space=pltpu.VMEM)
+    arrived = pl.pallas_call(
+        lambda *refs: spread_kernel(group, *refs),
+        in_specs=[whole],
+        out_specs=whole,
+        out_shape=jax.ShapeDtypeStruct(flat.shape, flat.dtype),
+        scratch_shapes=[pltpu.SemaphoreType.DMA((group - 1,))] * 2,
+        compiler_params=pltpu.CompilerParams(
+            collective_id=1, has_side_effects=True, vmem_limit_bytes=32 * 1024 * 1024
+        ),
+        name="spread",
+    )(flat)
+    return arrived.reshape(pieces.shape)
+
+
 def shift_rows(field, offset, sign):
     count = lax.axis_size("gx")
     for bit_pos in range(3):
@@ -229,14 +276,6 @@
         moved = lax.ppermute(field, "gx", [(i, (i + by) % count) for i in range(count)])
         field = jnp.where(offset >> bit_pos & 1 == 1, moved, field)
     return field
-
-
-def exchange(pieces, group):
-    count = lax.axis_size("gx")
-    groups = None
-    if count != group:
-        groups = [list(range(i, i + group)) for i in range(0, count, group)]
-    return lax.all_to_all(pieces, "gx", 0, 0, axis_index_groups=groups, tiled=True)
 
 
 def per_device(tokens, cotangent, offsets, norm_gain, qkv_weight, proj_weight):
@@ -250,7 +289,7 @@
         offsets = offsets * jnp.array([0, 1, 1], offsets.dtype)
     stacked = jnp.roll(stacked, -offsets[2], axis=2)
     pieces = stacked.reshape(2, extent_y, group, W, features).transpose(2, 0, 1, 3, 4)
-    data = exchange(pieces, group)
+    data = spread(pieces, group)
     grads, acc = windows_back(offsets, data, norm_gain, qkv_weight, proj_weight)
     back, total = return_and_sum(grads, acc, group)
     field = back.transpose(1, 0, 2, 3).reshape(1, extent_y, extent_z, features)

time: 95.4 us -> 93.1 us (0.976)
  Pallas kernels: 54.9 us -> 82 us
  waiting for transfers between devices: 21.5 us -> 0 us
  starting transfers between devices: 7.49 us -> 0 us
  other arithmetic: 4.22 us -> 3.17 us
    pallas_call x0 -> x1, Pallas kernels: none -> 23 us  [spread(): pl.pallas_call(lambda *refs: spread_kernel(group, *refs), in_specs=[whole...]
    all_to_all x1 -> x0, waiting for transfers between devices: 21.5 us -> none  [exchange(): lax.all_to_all(pieces, 'gx', 0, 0, axis_index_groups=groups, tiled=True)]
    all_to_all x1 -> x0, starting transfers between devices: 7.49 us -> none  [exchange(): lax.all_to_all(pieces, 'gx', 0, 0, axis_index_groups=groups, tiled=True)]
    pallas_call x1, Pallas kernels: 30.9 us -> 35 us  [return_and_sum(): pl.pallas_call(lambda *refs: return_kernel(group, *refs), in_specs=[whole...]
    transpose x1, other arithmetic: 3 us -> 1.95 us  [per_device(): stacked.reshape(2, extent_y, group, W, features).transpose(2, 0, 1, 3, 4)]
  transfers between devices with their start and end apart: 1 -> 0, of which waited for: 1 -> 0; matrix products, arithmetic and copies ran while one was open for 0% -> 0% of each run, Pallas kernels for 0% -> 0%
where the time goes in v4:
time: 93.1 us; the launch traced here: 92.3 us
  Pallas kernels  82 us (88%)
  local copies, waits for them, and re-layouts  3.75 us (4%)
  between operations  3.4 us (4%)
  other arithmetic  3.17 us (3%)
    pallas_call x1, Pallas kernels, return_and_sum(): pl.pallas_call(lambda *refs: return_kernel(group, *refs), in_specs=[whole...  35 us
    pallas_call x1, Pallas kernels, windows_back(): pl.pallas_call(window_kernel, grid=(steps,), in_specs=[pl.BlockSpec(memor...  24 us
    pallas_call x1, Pallas kernels, spread(): pl.pallas_call(lambda *refs: spread_kernel(group, *refs), in_specs=[whole...  23 us
    transpose x1, other arithmetic, per_device(): stacked.reshape(2, extent_y, group, W, features).transpose(2, 0, 1, 3, 4)  1.95 us

profile of v4, /device:TPU:1, one launch (start us, length us, event | category | flops | bytes accessed | tf_op | source)
XLA Modules:
  0.0 92.3 jit_solution(4480868037309406731)
XLA Ops:
  0.6 1.2 %slice.16 = s32[1]{0:T(128)} slice(s32[3]{0:T(128)} %offsets_ref.1), slice={[2:3]} | slice | bytes 8 | tf_op jit(solution)/shard_map/slice | solution.py:290
  4.5 1.9 %fusion.2 = bf16[16,2,16,8,128]{4,3,0,2,1:T(8,128)(2,1)S(1)} fusion(s32[]{:T(128)S(6)} %select_n.33, bf16[1,16,128,128]{3,2,1,0:T(8,128)(2,1)} %param.6, bf16[1,16,128,128]{3,2,1,0:T(8,128)(2,1)} %param.7), kind=kLoop, calls=%fused_computation.6 | loop fusion | flops 4194304 | bytes 2097156 | tf_op jit(solution)/shard_map/transpose | solution.py:291
  6.4 0.3 copy.13
  6.7 0.0 copy-start
  6.7 0.0 copy-start.3
  6.8 0.0 copy-start.1
  6.8 0.0 copy-start.2
  6.8 23.0 %spread.1 = bf16[16,256,128]{2,1,0:T(8,128)(2,1)S(1)} custom-call(bf16[16,256,128]{2,1,0:T(8,128)(2,1)S(1)} %bitcast.23), custom_call_target="tpu_custom_call" | custom-call | tf_op jit(solution)/shard_map/spread/pallas_call | solution.py:258
  29.8 0.0 copy-done
  29.8 0.1 copy.14
  29.9 0.0 copy-done.3
  29.9 0.1 copy.15
  30.1 0.0 copy-done.1
  30.1 0.0 copy-done.2
  30.1 24.0 %shard_map.93 = (bf16[16,16,8,128]{3,2,1,0:T(8,128)(2,1)S(1)}, f32[128,640]{1,0:T(8,128)S(1)}) custom-call(s32[3]{0:T(128)S(1)} %copy-done.1, bf16[16,2,16,8,128]{4,3,2,1,0:T(8,128)(2,1)S(1)} %bitcast.24, f32[1,128]{1,0:T(1,128)S(1)} %bitcast.28, bf16[128,384]{1,0:T(8,128)(2,1)S(1)} %copy-done, bf16[640,128]{1,0:T(8,128)(2,1)S(1)} %pad_maximum_fusion.back_ref, ...), custom_call_target="tpu_custom_call" | custom-call | flops 1610612736 | bytes 1572864 | tf_op jit(solution)/shard_map/pallas_call | solution.py:132
  54.2 35.0 %return_and_sum.1 = (bf16[16,128,128]{2,1,0:T(8,128)(2,1)S(1)}, f32[16,8,640]{2,1,0:T(8,128)S(1)}) custom-call(bf16[16,128,128]{2,1,0:T(8,128)(2,1)S(1)} %bitcast.25, f32[16,8,640]{2,1,0:T(8,128)S(1)} %bitcast.26), custom_call_target="tpu_custom_call" | custom-call | tf_op jit(solution)/shard_map/return_and_sum/pallas_call | solution.py:204
  89.2 0.1 copy_bitcast_fusion
  89.3 1.2 %fusion.4 = bf16[1,16,128,128]{3,2,1,0:T(8,128)(2,1)} fusion(s32[]{:T(128)S(6)} %select_n.36, bf16[1,16,128,128]{3,2,1,0:T(8,128)(2,1)S(1)} %copy_bitcast_fusion), kind=kLoop, calls=%fused_computation.10 | loop fusion | flops 1048576 | bytes 1048580 | tf_op jit(solution)/shard_map/jit(_roll_dynamic)/concatenate | solution.py:296
  90.5 0.7 slice.22
  91.2 0.6 slice.23
  91.8 0.5 slice_bitcast_fusion
  (5 shorter events, 0.1 us)
Async XLA Ops:
  6.7 23.0 %copy-start = (bf16[128,384]{1,0:T(8,128)(2,1)S(1)}, bf16[128,384]{1,0:T(8,128)(2,1)}, u32[]{:S(2)}) copy-start(bf16[128,384]{1,0:T(8,128)(2,1)} %qkv_ref.1) | copy-start | bytes 294916
  6.7 23.2 %copy-start.3 = (bf16[128,128]{1,0:T(8,128)(2,1)S(1)}, bf16[128,128]{1,0:T(8,128)(2,1)}, u32[]{:S(2)}) copy-start(bf16[128,128]{1,0:T(8,128)(2,1)} %param.11) | copy-start | bytes 98308
  6.8 23.3 %copy-start.1 = (s32[3]{0:T(128)S(1)}, s32[3]{0:T(128)}, u32[]{:S(2)}) copy-start(s32[3]{0:T(128)} %offsets_ref.1) | copy-start | bytes 40
  6.8 23.3 %copy-start.2 = (f32[128]{0:T(128)S(1)}, f32[128]{0:T(128)}, u32[]{:S(2)}) copy-start(f32[128]{0:T(128)} %param.9) | copy-start | bytes 1540
